TPU v7x, 128 devices: a whole 4x4x4 slice. The times are simulated.
128 devices in a mesh: table: 8 (over y, core), dom: 16 (over z, x).
Axes of the slice: x: 4, y: 4, z: 4, core: 2. Of those that a mesh axis runs over, the one named last changes fastest.
Arguments:
- tables: float32 [8, 131072, 128], P('table', 'dom'), may hold values from -6 to 6
- owner_ids: int32 [65536, 4], P(('table', 'dom')), may hold values from 0 to 127, all different within a row; in each aligned block of 512 rows (0 to 511, 512 to 1023, ...) at most 32 rows name the same one
- row_ids: int32 [65536, 4], P(('table', 'dom')), may hold values from 0 to 8191
- neighbour_part: int32 [512, 4], P(('table', 'dom')), may hold values from 0 to 15, all different within a row; in each aligned block of 4 rows (0 to 3, 4 to 7, ...) at most 2 rows name the same one
- neighbour_block: int32 [512, 4], P(('table', 'dom')), may hold values from 0 to 3
- adjacency: bfloat16 [512, 4, 128, 128], P(('table', 'dom')), may hold values from 0.001 to 1.81
- w_in: bfloat16 [128, 1024], replicated, may hold values from -0.5 to 0.5
- w_pool: bfloat16 [1024, 1024], replicated, may hold values from -0.1875 to 0.1875
- w_self: bfloat16 [1024, 1024], replicated, may hold values from -0.1875 to 0.1875
- w_neigh: bfloat16 [1024, 1024], replicated, may hold values from -0.75 to 0.75
- out_gain: bfloat16 [1024], replicated, may hold values from 0.25 to 1.75
- cotangent: bfloat16 [65536, 1024], P(('table', 'dom')), may hold values from -6 to 6
Outputs:
- node_out: bfloat16 [65536, 1024], P(('table', 'dom'))
- table_grad: float32 [8, 131072, 128], P('table', 'dom')
Inputs may be any that keep to these rules, and one draw needn't show every extreme that they name: `owner_ids`: the 4 entries of a row differ. Among the 512 rows of one device no owner is named more than 32 times, and in some device's rows some owner is named exactly 32 times. `neighbour_part`: the 4 entries of a row differ. Among the 4 rows of one device no partition is named more than 2 times, and in some device's rows some partition is named exactly 2 times.
All inputs are finite; a program needn't handle non-finite values.
Results may differ from a plain program's by a relative error of at most 0.012.
Values may be sent and summed in bfloat16 or wider, within the bound.
A program may use at most 128 MiB of HBM per device.

v0:
```python
import jax
import jax.numpy as jnp
from jax import lax
from jax.sharding import PartitionSpec as P

EPSILON = 1e-06


def split_up(array, dim, peers):
    before, after = (array.shape[:dim], array.shape[dim + 1 :])
    return jnp.moveaxis(array.reshape(*before, peers, -1, *after), dim, 0)


def in_order(parts, dim):
    shape = list(parts.shape[1:])
    shape[dim] *= parts.shape[0]
    return jnp.moveaxis(parts, 0, dim).reshape(shape)


def joined_exchange(array, axis, axes, splits, concats):
    sizes = [lax.axis_size(a) for a in axes]
    parts = split_up(array, splits[0], sizes[0])
    parts = jnp.moveaxis(split_up(parts, splits[1] + 1, sizes[1]), 0, 1)
    inside = parts.shape[2:]
    parts = parts.reshape(-1, *inside)
    parts = lax.all_to_all(parts, axis, split_axis=0, concat_axis=0, tiled=True)
    parts = in_order(parts.reshape(*sizes, *inside), concats[0] + 1)
    return in_order(parts, concats[1])


def silu_slope(inputs):
    sigmoid_part = jax.nn.sigmoid(inputs)
    return sigmoid_part * (1.0 + inputs * (1.0 - sigmoid_part))


def times_transpose(left_side, right_side):
    return lax.dot_general(
        left_side, right_side, (((1,), (1,)), ((), ())), preferred_element_type=jnp.float32
    )


def bucket_slots(target, buckets, capacity):
    onehot = (target[:, None] == jnp.arange(buckets, dtype=jnp.int32)[None, :]).astype(jnp.int32)
    before = jnp.cumsum(onehot, axis=0) - onehot
    position = jnp.sum(before * onehot, axis=1)
    return target * capacity + position


def request_swap(buffer):
    shaped = buffer.reshape((lax.axis_size("table"), lax.axis_size("dom")) + buffer.shape[1:])
    moved = joined_exchange(shaped, ("table", "dom"), ("table", "dom"), (0, 1), (0, 1))
    return moved.reshape(buffer.shape)


def row_swap(buffer):
    shaped = buffer.reshape((lax.axis_size("table"), lax.axis_size("dom")) + buffer.shape[1:])
    moved = joined_exchange(
        shaped.astype(jnp.bfloat16), ("table", "dom"), ("table", "dom"), (0, 1), (0, 1)
    ).astype(shaped.dtype)
    return moved.reshape(buffer.shape)


def body(
    tables,
    owner_ids,
    row_ids,
    neighbour_part,
    neighbour_block,
    adjacency,
    w_in,
    w_pool,
    w_self,
    w_neigh,
    out_gain,
    cotangent,
):
    groups = lax.axis_size("table")
    domains = lax.axis_size("dom")
    devices = groups * domains
    node_count, lookup_count = owner_ids.shape
    table_width = tables.shape[2]
    rows_local = tables.shape[1]
    hidden_width = w_self.shape[0]
    capacity = max(2, (2 * node_count * lookup_count + devices - 1) // devices)
    row_slots = bucket_slots(owner_ids.reshape(-1), devices, capacity)
    requests = jnp.full((devices * capacity,), -1, jnp.int32).at[row_slots].set(row_ids.reshape(-1))
    incoming = request_swap(requests.reshape(devices, capacity))
    present = incoming >= 0
    safe_rows = jnp.where(present, incoming, 0)
    fetched = jnp.where(present[:, :, None], tables[0][safe_rows], 0.0)
    returned = row_swap(fetched)
    looked = returned.reshape(devices * capacity, table_width)[row_slots].reshape(
        node_count, lookup_count, table_width
    )
    feature = jnp.sum(looked, axis=1).astype(jnp.bfloat16)
    hidden = jnp.dot(feature, w_in, preferred_element_type=jnp.float32).astype(jnp.bfloat16)
    pooled_pre = jnp.dot(hidden, w_pool, preferred_element_type=jnp.float32)
    pooled = jax.nn.silu(pooled_pre).astype(jnp.bfloat16)
    block_rows = adjacency.shape[-1]
    block_count = node_count // block_rows
    fanout = neighbour_part.shape[1]
    halo_cap = max(2, (2 * block_count * fanout + domains - 1) // domains)
    halo_slots = bucket_slots(neighbour_part.reshape(-1), domains, halo_cap)
    wanted = (
        jnp.full((domains * halo_cap,), -1, jnp.int32)
        .at[halo_slots]
        .set(neighbour_block.reshape(-1))
    )
    asked_blocks = lax.all_to_all(
        wanted.reshape(domains, halo_cap), "dom", split_axis=0, concat_axis=0, tiled=True
    )
    gathered = lax.all_gather(pooled, "dom", axis=0, tiled=True)
    flat_index = neighbour_part.reshape(-1) * block_count + neighbour_block.reshape(-1)
    sources = gathered.reshape(domains * block_count, block_rows, hidden_width)[flat_index]
    sources = sources.reshape(block_count, fanout, block_rows, hidden_width)
    inverse = 1.0 / jnp.sum(adjacency.astype(jnp.float32), axis=(1, 3))
    summed = jnp.einsum("bkij,bkjh->bih", adjacency, sources, preferred_element_type=jnp.float32)
    neighbour_mean = (
        (summed * inverse[:, :, None]).astype(jnp.bfloat16).reshape(node_count, hidden_width)
    )
    pre_act = jnp.dot(hidden, w_self, preferred_element_type=jnp.float32) + jnp.dot(
        neighbour_mean, w_neigh, preferred_element_type=jnp.float32
    )
    active = jax.nn.silu(pre_act)
    rms_scale = lax.rsqrt(jnp.mean(active * active, axis=1, keepdims=True) + EPSILON)
    gain_wide = out_gain.astype(jnp.float32)
    node_out = (active * rms_scale * gain_wide).astype(jnp.bfloat16)
    weighted = gain_wide * cotangent.astype(jnp.float32)
    d_active = rms_scale * weighted - active * (rms_scale * rms_scale * rms_scale) * jnp.mean(
        weighted * active, axis=1, keepdims=True
    )
    d_pre = (d_active * silu_slope(pre_act)).astype(jnp.bfloat16)
    d_hidden_self = times_transpose(d_pre, w_self)
    d_mean = times_transpose(d_pre, w_neigh)
    d_scaled = (d_mean.reshape(block_count, block_rows, hidden_width) * inverse[:, :, None]).astype(
        jnp.bfloat16
    )
    shares = jnp.einsum(
        "bkij,bih->bkjh", adjacency, d_scaled, preferred_element_type=jnp.float32
    ).astype(jnp.bfloat16)
    outgoing = (
        jnp.zeros((domains * halo_cap, block_rows, hidden_width), jnp.bfloat16)
        .at[halo_slots]
        .set(shares.reshape(block_count * fanout, block_rows, hidden_width))
    )
    back_grads = lax.all_to_all(
        outgoing.reshape(domains, halo_cap, block_rows, hidden_width),
        "dom",
        split_axis=0,
        concat_axis=0,
        tiled=True,
    )
    target_blocks = jnp.where(asked_blocks >= 0, asked_blocks, block_count).reshape(-1)
    d_pooled = (
        jnp.zeros((block_count, block_rows, hidden_width), jnp.float32)
        .at[target_blocks]
        .add(
            back_grads.reshape(domains * halo_cap, block_rows, hidden_width).astype(jnp.float32),
            mode="drop",
        )
    )
    d_pool_pre = (d_pooled.reshape(node_count, hidden_width) * silu_slope(pooled_pre)).astype(
        jnp.bfloat16
    )
    d_hidden = (d_hidden_self + times_transpose(d_pool_pre, w_pool)).astype(jnp.bfloat16)
    d_feature = times_transpose(d_hidden, w_in)
    spread = jnp.broadcast_to(
        d_feature[:, None, :], (node_count, lookup_count, table_width)
    ).reshape(node_count * lookup_count, table_width)
    outgoing_rows = (
        jnp.zeros((devices * capacity, table_width), jnp.float32).at[row_slots].set(spread)
    )
    owed_grads = row_swap(outgoing_rows.reshape(devices, capacity, table_width))
    grad_rows = jnp.where(present, incoming, rows_local).reshape(-1)
    table_grad = (
        jnp.zeros((rows_local, table_width), jnp.float32)
        .at[grad_rows]
        .add(owed_grads.reshape(devices * capacity, table_width), mode="drop")
    )
    return (node_out, table_grad[None])


def solution(mesh):
    placed = (
        P("table", "dom", None),
        P(("table", "dom"), None),
        P(("table", "dom"), None),
        P(("table", "dom"), None),
        P(("table", "dom"), None),
        P(("table", "dom"), None, None, None),
        P(),
        P(),
        P(),
        P(),
        P(),
        P(("table", "dom"), None),
    )
    return jax.shard_map(
        body,
        mesh=mesh,
        in_specs=placed,
        out_specs=(P(("table", "dom"), None), P("table", "dom", None)),
        check_vma=False,
    )
```

profile of v0, /device:TPU:1, one launch (start us, length us, event | category | flops | bytes accessed | tf_op | source)
XLA Modules:
  0.0 500.0 jit_solution(11178647670998931295)
XLA Ops:
  11.5 8.1 %scatter_custom_fusion = s32[4096]{0:T(1024)S(1)} fusion(s32[2048]{0:T(1024)S(1)} %bitcast.137, s32[2048]{0:T(1024)S(1)} %reshape.372, s32[]{:T(128)} %constant.13.clone.1), kind=kCustom, calls=%fused_computation.60 | custom fusion | bytes 16388 | tf_op jit(solution)/shard_map/scatter | solution.py:86
  19.6 21.1 %all_to_all.32 = s32[128,1,1,32]{3,2,1,0:T(1,128)S(1)} all-to-all(s32[128,1,1,32]{3,2,1,0:T(1,128)S(1)} %bitcast.134), channel_id=1, replica_groups=mesh['table'=8,'dom'=16] {'table','dom'}, dimensions={0} | all-to-all | bytes 32768 | tf_op jit(solution)/shard_map/all_to_all | solution.py:26
  40.8 13.2 %gather_fusion = bf16[4096,128]{1,0:T(8,128)(2,1)S(1)} fusion(f32[8192,128]{1,0:T(8,128)} %bitcast.120, s32[4096]{0:T(1024)S(1)} %broadcast_clamp_fusion), kind=kCustom, calls=%fused_computation | custom fusion | bytes 2113536 | tf_op jit(solution)/shard_map/gather | solution.py:90
  54.0 2.1 select_convert_fusion
  56.2 4.3 all-to-all-start.1
  60.5 19.3 %all-to-all-done.1 = bf16[128,1,1,32,128]{4,3,2,1,0:T(8,128)(2,1)S(1)} async-done(((bf16[128,1,1,32,128]{4,3,2,1,0:T(8,128)(2,1)}), bf16[128,1,1,32,128]{4,3,2,1,0:T(8,128)(2,1)S(1)}, u32[]{:S(2)}, u32[]{:S(2)}) %all-to-all-start.1) | async-done | bytes 1048608 | tf_op jit(solution)/shard_map/all_to_all | solution.py:26
  81.3 7.0 %gather_fusion.1 = f32[2048,128]{1,0:T(8,128)S(1)} fusion(f32[4096,128]{1,0:T(8,128)} %bitcast_convert_fusion.1, s32[2048]{0:T(1024)S(1)} %broadcast_clamp_fusion.1), kind=kCustom, calls=%fused_computation.1 | custom fusion | bytes 2105344 | tf_op jit(solution)/shard_map/gather | solution.py:92
  90.5 3.1 multiply_convert_fusion.3
  95.5 3.6 all-to-all-start.2
  99.4 4.8 fusion.26
  104.2 96.6 %all-gather.2.cloned.1.call-done = bf16[8192,1024]{1,0:T(8,128)(2,1)} async-done(((bf16[512,1024]{1,0:T(8,128)(2,1)}), bf16[8192,1024]{1,0:T(8,128)(2,1)}) %all-gather.2.cloned.1.call-update) | async-done | bytes 16777232 | tf_op jit(solution)/shard_map/all_gather | solution.py:112
  200.8 8.6 %gather_fusion.2 = bf16[16,128,1024]{2,1,0:T(8,128)(2,1)} fusion(bf16[64,128,1024]{2,1,0:T(8,128)(2,1)} %bitcast.132, s32[1024]{0:T(1024)S(1)} %pad_clamp_fusion), kind=kCustom, calls=%fused_computation.2 | custom fusion | bytes 8388672 | tf_op jit(solution)/shard_map/gather | solution.py:114
  209.4 3.1 fusion.3
  215.2 2.4 multiply_convert_fusion.1
  217.7 2.6 fusion.28
  220.3 2.9 copy.32
  223.2 4.8 convolution_convert_fusion
  228.1 6.4 %copy.33 = bf16[16,128,1024]{2,1,0:T(8,128)(2,1)} copy(bf16[16,128,1024]{1,2,0:T(8,128)(2,1)} %bitcast.121) | data formatting | bytes 8388608 | tf_op jit(solution)/shard_map/reshape | solution.py:144
  234.4 4.3 broadcast_in_dim.72
  238.7 10.9 %scatter_fusion = bf16[32,128,1024]{2,1,0:T(8,128)(2,1)} fusion(bf16[32,128,1024]{2,1,0:T(8,128)(2,1)} %broadcast_in_dim.72, s32[16]{0:T(128)S(1)} %fusion.22, bf16[16,128,1024]{2,1,0:T(8,128)(2,1)} %copy.33), kind=kCustom, calls=%fused_computation.5 | custom fusion | bytes 12582976 | tf_op jit(solution)/shard_map/scatter | solution.py:144
  249.6 5.2 %all-to-all-start.3 = ((bf16[16,2,128,1024]{3,2,1,0:T(8,128)(2,1)}), bf16[16,2,128,1024]{3,2,1,0:T(8,128)(2,1)}, u32[]{:S(2)}, u32[]{:S(2)}) async-start(bf16[16,2,128,1024]{3,2,1,0:T(8,128)(2,1)} %bitcast.119), calls=%async_computation.3 | async-start | bytes 16777216 | tf_op jit(solution)/shard_map/all_to_all | solution.py:146
  256.1 4.2 fusion.27
  260.3 117.7 %all-to-all-done.3 = bf16[16,2,128,1024]{3,2,1,0:T(8,128)(2,1)} async-done(((bf16[16,2,128,1024]{3,2,1,0:T(8,128)(2,1)}), bf16[16,2,128,1024]{3,2,1,0:T(8,128)(2,1)}, u32[]{:S(2)}, u32[]{:S(2)}) %all-to-all-start.3) | async-done | bytes 8388640 | tf_op jit(solution)/shard_map/all_to_all | solution.py:146
  378.0 11.3 %bitcast_convert_fusion = f32[32,128,1024]{2,1,0:T(8,128)} fusion(bf16[16,2,128,1024]{3,2,1,0:T(8,128)(2,1)} %all-to-all-done.3), kind=kLoop, calls=%fused_computation.9 | loop fusion | flops 4194304 | bytes 25165824 | tf_op jit(solution)/shard_map/convert_element_type | solution.py:158
  390.9 33.0 %scatter_fusion.1 = f32[4,128,1024]{2,1,0:T(8,128)} fusion(f32[4,128,1024]{2,1,0:T(8,128)} %broadcast_in_dim.40, s32[32]{0:T(128)S(1)} %fusion.23, f32[32,128,1024]{2,1,0:T(8,128)} %bitcast_convert_fusion), kind=kCustom, calls=%fused_computation.6 | custom fusion | flops 4194304 | bytes 50331776 | tf_op jit(solution)/shard_map/scatter-add | solution.py:157
  423.9 3.0 fusion.2
  426.9 3.3 fusion.6
  430.3 7.0 %scatter_custom_fusion.4 = f32[4096,128]{1,0:T(8,128)} fusion(s32[2048]{0:T(1024)S(1)} %bitcast.139, f32[2048,128]{1,0:T(8,128)S(1)} %bitcast.128, f32[]{:T(128)} %constant.18.clone.1), kind=kCustom, calls=%fused_computation.39 | custom fusion | bytes 2097156 | tf_op jit(solution)/shard_map/scatter | solution.py:171
  437.3 2.7 convert_element_type.142
  440.0 9.3 %all-to-all-start.4 = ((bf16[128,1,1,32,128]{4,3,2,1,0:T(8,128)(2,1)}), bf16[128,1,1,32,128]{4,3,2,1,0:T(8,128)(2,1)S(1)}, u32[]{:S(2)}, u32[]{:S(2)}) async-start(bf16[128,1,1,32,128]{4,3,2,1,0:T(8,128)(2,1)} %bitcast.45), calls=%async_computation.4 | async-start | bytes 2097152 | tf_op jit(solution)/shard_map/all_to_all | solution.py:26
  449.4 19.2 %all-to-all-done.4 = bf16[128,1,1,32,128]{4,3,2,1,0:T(8,128)(2,1)S(1)} async-done(((bf16[128,1,1,32,128]{4,3,2,1,0:T(8,128)(2,1)}), bf16[128,1,1,32,128]{4,3,2,1,0:T(8,128)(2,1)S(1)}, u32[]{:S(2)}, u32[]{:S(2)}) %all-to-all-start.4) | async-done | bytes 1048608 | tf_op jit(solution)/shard_map/all_to_all | solution.py:26
  468.6 24.6 %scatter_custom_fusion.5 = f32[8192,128]{1,0:T(8,128)} fusion(s32[4096]{0:T(1024)S(1)} %bitcast.140, bf16[4096,128]{1,0:T(8,128)(2,1)S(1)} %bitcast.125, f32[]{:T(128)} %constant.18.clone.1), kind=kCustom, calls=%fused_computation.11 | custom fusion | flops 1048576 | bytes 5242884 | tf_op jit(solution)/shard_map/scatter-add | solution.py:178
  (79 shorter events, 16.1 us)
Async XLA Ops:
  7.2 83.3 %copy-start = (bf16[1024,1024]{1,0:T(8,128)(2,1)S(1)}, bf16[1024,1024]{1,0:T(8,128)(2,1)}, u32[]{:S(2)}) copy-start(bf16[1024,1024]{1,0:T(8,128)(2,1)} %param.19) | copy-start | bytes 6291460
  9.7 0.8 copy-start.6
  56.2 23.6 %all-to-all-start.1 = ((bf16[128,1,1,32,128]{4,3,2,1,0:T(8,128)(2,1)}), bf16[128,1,1,32,128]{4,3,2,1,0:T(8,128)(2,1)S(1)}, u32[]{:S(2)}, u32[]{:S(2)}) async-start(bf16[128,1,1,32,128]{4,3,2,1,0:T(8,128)(2,1)} %select_convert_fusion), calls=%async_computation.1 | async-start | bytes 2097152 | tf_op jit(solution)/shard_map/all_to_all | solution.py:26
  60.4 140.4 %all-gather.2.cloned.1.call-start = ((), (), s32[]{:S(2)}) async-start(), calls=%async_computation.5 | async-start | bytes 17825792 | tf_op jit(solution)/shard_map/all_gather | solution.py:112
  90.4 3.1 copy-start.5
  90.4 3.2 copy-start.7
  90.5 3.4 copy-start.8
  90.5 8.7 %copy-start.9 = (bf16[1024]{0:T(1024)(128)(2,1)S(1)}, bf16[1024]{0:T(1024)(128)(2,1)}, u32[]{:S(2)}) copy-start(bf16[1024]{0:T(1024)(128)(2,1)} %param.22) | copy-start | bytes 6148
  90.5 8.8 %copy-start.1 = (bf16[4,4,128,128]{3,2,1,0:T(8,128)(2,1)S(1)}, bf16[4,4,128,128]{3,2,1,0:T(8,128)(2,1)}, u32[]{:S(2)}) copy-start(bf16[4,4,128,128]{3,2,1,0:T(8,128)(2,1)} %param.17) | copy-start | bytes 1572868
  95.5 154.1 %all-to-all-start.2 = ((s32[16,1,2]{2,1,0:T(1,128)}), s32[16,1,2]{2,1,0:T(1,128)S(1)}, u32[]{:S(2)}, u32[]{:S(2)}) async-start(s32[16,1,2]{2,1,0:T(1,128)} %bitcast.34), calls=%async_computation.2 | async-start | bytes 16384 | tf_op jit(solution)/shard_map/all_to_all | solution.py:109
  209.4 3.1 copy-start.2
  209.4 3.2 copy-start.10
  209.4 3.8 copy-start.11
  217.7 2.6 copy-start.3
  249.6 6.5 %copy-start.4 = (bf16[512,1024]{1,0:T(8,128)(2,1)S(1)}, bf16[512,1024]{1,0:T(8,128)(2,1)}, u32[]{:S(2)}) copy-start(bf16[512,1024]{1,0:T(8,128)(2,1)} %copy-done.3) | copy-start | bytes 3145732
  249.6 128.4 %all-to-all-start.3 = ((bf16[16,2,128,1024]{3,2,1,0:T(8,128)(2,1)}), bf16[16,2,128,1024]{3,2,1,0:T(8,128)(2,1)}, u32[]{:S(2)}, u32[]{:S(2)}) async-start(bf16[16,2,128,1024]{3,2,1,0:T(8,128)(2,1)} %bitcast.119), calls=%async_computation.3 | async-start | bytes 16777216 | tf_op jit(solution)/shard_map/all_to_all | solution.py:146
  440.0 28.6 %all-to-all-start.4 = ((bf16[128,1,1,32,128]{4,3,2,1,0:T(8,128)(2,1)}), bf16[128,1,1,32,128]{4,3,2,1,0:T(8,128)(2,1)S(1)}, u32[]{:S(2)}, u32[]{:S(2)}) async-start(bf16[128,1,1,32,128]{4,3,2,1,0:T(8,128)(2,1)} %bitcast.45), calls=%async_computation.4 | async-start | bytes 2097152 | tf_op jit(solution)/shard_map/all_to_all | solution.py:26
Sparse Core Ops, SparseCore 0:
  93.7 107.0 all-gather.1
where the time goes:
time: 501 us; the launch traced here: 500 us
  waiting for transfers between devices  253 us (50%)
  other arithmetic  84.3 us (17%)
  local copies, waits for them, and re-layouts  75.8 us (15%)
  matrix products  29.2 us (6%)
  starting transfers between devices  22.4 us (4%)
  blocking collectives  21.1 us (4%)
  between operations  14.4 us (3%)
    all_to_all x1, waiting for transfers between devices, body(): lax.all_to_all(outgoing.reshape(domains, halo_cap, block_rows, hidden_wid...  118 us
    all_gather x1, waiting for transfers between devices, body(): gathered = lax.all_gather(pooled, 'dom', axis=0, tiled=True)  96.6 us
    all_to_all x2, waiting for transfers between devices, joined_exchange(): parts = lax.all_to_all(parts, axis, split_axis=0, concat_axis=0, tiled=True)  38.4 us
    scatter-add x1, other arithmetic, body(): d_pooled = jnp.zeros((block_count, block_rows, hidden_width), jnp.float32...  33 us
    scatter-add x1, other arithmetic, body(): table_grad = jnp.zeros((rows_local, table_width), jnp.float32).at[grad_ro...  24.6 us
    all_to_all x1, blocking collectives, joined_exchange(): parts = lax.all_to_all(parts, axis, split_axis=0, concat_axis=0, tiled=True)  21.1 us
    all_to_all x2, starting transfers between devices, joined_exchange(): parts = lax.all_to_all(parts, axis, split_axis=0, concat_axis=0, tiled=True)  13.5 us
    gather x1, local copies, waits for them, and re-layouts, body(): fetched = jnp.where(present[:, :, None], tables[0][safe_rows], 0.0)  13.2 us
  transfers between devices with their start and end apart: 5, of which 4 were waited for; matrix products, arithmetic and copies ran while one was open for 12% of the time, Pallas kernels for 0%

commit v1 on v0

v1 whole, which is shorter than its diff:
```python
import jax
import jax.numpy as jnp
from jax import lax
from jax.experimental import pallas as pl
from jax.experimental.pallas import tpu as pltpu
from jax.sharding import PartitionSpec as P

EPSILON = 1e-06
MESH = pl.DeviceIdType.MESH
F32 = jnp.float32
BF16 = jnp.bfloat16
LIMIT = 60 * 1024 * 1024


def iota(shape, dim):
    return lax.broadcasted_iota(jnp.int32, shape, dim)


def dot(a, b, dims=((1,), (0,))):
    return lax.dot_general(a, b, (dims, ((), ())), preferred_element_type=F32)


def everyone(act):
    table, dom = lax.axis_index("table"), lax.axis_index("dom")
    for step in range(8):
        there = lax.rem(table + step, 8)

        def body(k, carry):
            act(there, lax.rem(dom + k, 16))
            return carry

        lax.fori_loop(0 if step else 1, 16, body, 0)


def greet():
    barrier = pltpu.get_barrier_semaphore()
    everyone(
        lambda t, d: pl.semaphore_signal(barrier, inc=1, device_id=(t, d), device_id_type=MESH)
    )


def met():
    pl.semaphore_wait(pltpu.get_barrier_semaphore(), 127)


def swap_start(out_ref, in_ref, send, recv, local):
    table, dom = lax.axis_index("table"), lax.axis_index("dom")
    me = table * 16 + dom
    pltpu.make_async_copy(out_ref.at[me], in_ref.at[me], local).start()
    everyone(
        lambda t, d: pltpu.make_async_remote_copy(
            out_ref.at[t * 16 + d], in_ref.at[me], send, recv, device_id=(t, d), device_id_type=MESH
        ).start()
    )


def swap_wait(out_ref, in_ref, send, recv, local, others=127):
    table, dom = lax.axis_index("table"), lax.axis_index("dom")
    pltpu.make_async_copy(out_ref.at[0], in_ref.at[0], local).wait()
    whole = pltpu.make_async_remote_copy(
        out_ref.at[pl.ds(0, others)],
        in_ref.at[pl.ds(0, others)],
        send,
        recv,
        device_id=(table, lax.rem(dom + 1, 16)),
        device_id_type=MESH,
    )
    whole.wait_send()
    whole.wait_recv()


def gather_group(fa_ref, send, recv):
    table, dom = lax.axis_index("table"), lax.axis_index("dom")
    z, x = dom // 4, lax.rem(dom, 4)

    def place(h, i, j):
        dz, dx = (j, i) if h == 0 else (i, j)
        return lax.rem(z + dz + 4, 4) * 4 + lax.rem(x + dx + 4, 4)

    def copy(h, number, piece, start, count, to):
        blocks = fa_ref.at[pl.ds(place(h, *piece) * 4 + 2 * h + start, count)]
        return pltpu.make_async_remote_copy(
            blocks,
            blocks,
            send.at[h, number],
            recv.at[h, number],
            device_id=(table, place(h, *to)),
            device_id_type=MESH,
        )

    up, down = (1, 0), (-1, 0)
    away, back = (0, 1), (0, -1)
    pieces = (0, -1, 1, 2)
    first = (up, down)
    across = (away, back)
    sides = (0, 1)

    def near(h, side):
        return copy(h, side, (0, 0), 0, 2, first[side])

    def far(h, side):
        return copy(h, 2 + side, (2 * side - 1, 0), side, 1, first[side])

    def second(h, n, side):
        return copy(h, 4 + 4 * n + side, (pieces[n], 0), 0, 2, across[side])

    def second_far(h, n, side):
        return copy(h, 6 + 4 * n + side, (pieces[n], 2 * side - 1), side, 1, across[side])

    def near_in(h, side):
        return copy(h, side, (2 * side - 1, 0), 0, 2, first[side])

    def far_in(h, side):
        return copy(h, 2 + side, (2, 0), side, 1, first[side])

    def second_in(h, n, side):
        return copy(h, 4 + 4 * n + side, (pieces[n], 2 * side - 1), 0, 2, across[side])

    def second_far_in(h, n, side):
        return copy(h, 6 + 4 * n + side, (pieces[n], 2), side, 1, across[side])

    for h in range(2):
        for side in sides:
            near(h, side).start()
    for h in range(2):
        for side in sides:
            second(h, 0, side).start()
    for side in sides:
        for h in range(2):
            near_in(h, side).wait_recv()
            far(h, side).start()
            for other in sides:
                second(h, 1 + side, other).start()
    for side in sides:
        for h in range(2):
            second_in(h, 0, side).wait_recv()
            second_far(h, 0, side).start()
    for h in range(2):
        for side in sides:
            far_in(h, side).wait_recv()
        for side in sides:
            second(h, 3, side).start()
    for n in (1, 2, 3):
        for side in sides:
            for h in range(2):
                second_in(h, n, side).wait_recv()
                second_far(h, n, side).start()
    for h in range(2):
        for side in sides:
            near(h, side).wait_send()
            far(h, side).wait_send()
            for n in range(4):
                second_far_in(h, n, side).wait_recv()
                second(h, n, side).wait_send()
                second_far(h, n, side).wait_send()


def two_part(w_ref, product):
    high = product.astype(BF16)
    w_ref[0:128, :] = high
    w_ref[128:256, :] = (product - high.astype(F32)).astype(BF16)


def rows_asked(asked):
    above = pltpu.roll(asked, 96, 1)
    row = ((above - 1.0) * 128.0 + asked).astype(jnp.int32)
    low = row >> 10
    return row - low * 1024, low


def front_kernel(
    key_ref,
    key_t_ref,
    tables_ref,
    w_in_ref,
    w_pool_ref,
    w_self_ref,
    fa_ref,
    asked_ref,
    slot_t_ref,
    wip_ref,
    wis_ref,
    table,
    packed,
    request,
    slot,
    wide,
    out_rows,
    in_rows,
    onehot,
    high_b,
    low_b,
    select,
    ordered,
    load_sem,
    swap_sem,
    send,
    recv,
):
    greet()
    load = pltpu.make_async_copy(tables_ref, table, load_sem)
    load.start()
    key, key_t = key_ref[...], key_t_ref[...]
    owner, owner_t = key >> 13, key_t >> 13
    row = key - owner * 8192
    row_a = (row >> 7) + 1
    row_b = row - (row >> 7) * 128
    lanes = iota((512, 128), 1)
    subs = iota((128, 512), 0)
    hits = [jnp.where(owner[:, j : j + 1] == lanes, 1.0, 0.0) for j in range(4)]
    hits_t = [jnp.where(owner_t[j : j + 1, :] == subs, 1.0, 0.0) for j in range(4)]
    hit, hit_t = sum(hits), sum(hits_t)
    lower = jnp.where(iota((512, 512), 0) > iota((512, 512), 1), 1.0, 0.0).astype(BF16)
    upper = jnp.where(iota((512, 512), 0) < iota((512, 512), 1), 1.0, 0.0).astype(BF16)
    rank = dot(lower, hit.astype(BF16))
    rank_t = dot(hit_t.astype(BF16), upper)
    slot[...] = jnp.where(hit > 0.5, rank, -1.0)
    slot_t_ref[...] = jnp.where(hit_t > 0.5, rank_t, -1.0)
    asks = jnp.zeros((128, 128), F32)
    for j in range(4):
        position = jnp.sum(hits[j] * rank, axis=1, keepdims=True).astype(jnp.int32)
        value = jnp.where(lanes == position, row_b[:, j : j + 1].astype(F32), 0.0) + jnp.where(
            lanes == position + 32, row_a[:, j : j + 1].astype(F32), 0.0
        )
        asks = asks + dot(hits_t[j].astype(BF16), value.astype(BF16))
    request[...] = asks.reshape(128, 1, 128)
    met()
    swap_start(request, asked_ref, swap_sem.at[0], swap_sem.at[1], swap_sem.at[2])
    load.wait()
    for c in range(8):
        packed[:, c * 128 : (c + 1) * 128] = table[c * 1024 : (c + 1) * 1024, :].astype(BF16)
    two_part(wip_ref, dot(w_in_ref[...], w_pool_ref[...]))
    two_part(wis_ref, dot(w_in_ref[...], w_self_ref[...]))
    swap_wait(request, asked_ref, swap_sem.at[0], swap_sem.at[1], swap_sem.at[2])

    high, low = rows_asked(asked_ref[...].reshape(128, 128))
    for p in range(32):
        high_b[p] = jnp.broadcast_to(high[:, p : p + 1], (128, 128))
        low_b[p] = jnp.broadcast_to(low[:, p : p + 1], (128, 128))
    lane = iota((128, 128), 1)

    def lookup(g, carry):
        for q in range(8):
            h = high_b[g * 8 + q]
            for c in range(8):
                onehot[q * 128 : (q + 1) * 128, c * 128 : (c + 1) * 128] = jnp.where(
                    h == lane + c * 128, 1.0, 0.0
                ).astype(BF16)
        found = dot(onehot[...], packed[...])
        for q in range(8):
            l = low_b[g * 8 + q]
            total = jnp.zeros((128, 128), F32)
            for c in range(8):
                total = total + jnp.where(
                    l == c, found[q * 128 : (q + 1) * 128, c * 128 : (c + 1) * 128], 0.0
                )
            wide[pl.ds(g * 8 + q, 128, stride=32), :] = total
        return carry

    lax.fori_loop(0, 4, lookup, 0)
    out_rows[...] = wide[...].reshape(128, 32, 128).astype(BF16)
    swap_start(out_rows, in_rows, swap_sem.at[3], swap_sem.at[4], swap_sem.at[5])
    place = slot[...]
    for p in range(32):
        select[:, p * 128 : (p + 1) * 128] = jnp.where(place == float(p), 1.0, 0.0).astype(BF16)
    swap_wait(out_rows, in_rows, swap_sem.at[3], swap_sem.at[4], swap_sem.at[5])
    wide[...] = in_rows[...].astype(F32).reshape(4096, 128)
    for p in range(32):
        ordered[p * 128 : (p + 1) * 128, :] = wide[pl.ds(p, 128, stride=32), :].astype(BF16)
    feature = dot(select[...], ordered[...]).astype(BF16)
    fa_ref[pl.ds(lax.axis_index("dom") * 4, 4)] = feature.reshape(4, 128, 128)
    gather_group(fa_ref, send, recv)


def back_kernel(
    source_ref,
    pair_ref,
    block_ref,
    fa_ref,
    slot_t_ref,
    wip_ref,
    wis_ref,
    w_neigh_ref,
    gain_ref,
    adjacency_ref,
    cotangent_ref,
    node_out_ref,
    in_rows,
    stacked,
    pooled,
    slope,
    inverse,
    mean,
    pre_act,
    d_pre,
    d_scaled,
    d_self,
    parts,
    halo_out,
    halo_in,
    select,
    wide,
    out_rows,
    swap_sem,
):
    table, dom = lax.axis_index("table"), lax.axis_index("dom")
    greet()

    def forward(b, carry):
        for k in range(4):
            f = fa_ref[source_ref[b * 4 + k]]
            stacked[k * 128 : (k + 1) * 128, 0:128] = f
            stacked[k * 128 : (k + 1) * 128, 128:256] = f
        pre = dot(stacked[...], wip_ref[...])
        s = jax.nn.sigmoid(pre)
        pooled[...] = (pre * s).astype(BF16)
        slope[b] = s * (1.0 + pre * (1.0 - s))
        edges = jnp.concatenate([adjacency_ref[b, k] for k in range(4)], axis=1)
        inv = 1.0 / jnp.sum(edges.astype(F32), axis=1, keepdims=True)
        inverse[b] = jnp.broadcast_to(inv, (128, 128))
        mean[b] = (dot(edges, pooled[...]) * inv).astype(BF16)
        return carry

    lax.fori_loop(0, 4, forward, 0)
    own = fa_ref[pl.ds(dom * 4, 4)].reshape(512, 128)
    stacked[:, 0:128] = own
    stacked[:, 128:256] = own
    pre_act[...] = dot(stacked[...], wis_ref[...]) + dot(
        mean[...].reshape(512, 1024), w_neigh_ref[...]
    )
    gain = gain_ref[...].astype(F32)

    def norm(r, carry):
        rows = pl.ds(pl.multiple_of(r * 32, 32), 32)
        pre = pre_act[rows, :]
        s = jax.nn.sigmoid(pre)
        active = pre * s
        rms = lax.rsqrt(jnp.mean(active * active, axis=1, keepdims=True) + EPSILON)
        node_out_ref[rows, :] = (active * rms * gain).astype(BF16)
        weighted = gain * cotangent_ref[rows, :].astype(F32)
        d_active = rms * weighted - active * (rms * rms * rms) * jnp.mean(
            weighted * active, axis=1, keepdims=True
        )
        d_pre[rows, :] = (d_active * (s * (1.0 + pre * (1.0 - s)))).astype(BF16)
        return carry

    lax.fori_loop(0, 16, norm, 0)
    d_mean = dot(d_pre[...], w_neigh_ref[...], ((1,), (1,)))
    for b in range(4):
        d_scaled[b] = (d_mean[b * 128 : (b + 1) * 128, :] * inverse[b][:, 0:1]).astype(BF16)
    both = dot(d_pre[...], wis_ref[...], ((1,), (1,)))
    d_self[...] = (both[:, 0:128] + both[:, 128:256]).reshape(4, 128, 128)

    def backward(b, carry):
        edges = jnp.concatenate([adjacency_ref[b, k].T for k in range(4)], axis=0)
        d_pool = dot(edges, d_scaled[b]) * slope[b]
        pair = dot(d_pool.astype(BF16), wip_ref[...], ((1,), (1,)))
        parts[pl.ds(b * 4, 4)] = (
            (pair[:, 0:128] + pair[:, 128:256]).astype(BF16).reshape(4, 128, 128)
        )
        return carry

    lax.fori_loop(0, 4, backward, 0)
    tag_row = iota((16, 128), 0)

    def fill(q, carry):
        halo_out[q, 0:128, :] = parts[pair_ref[2 * q]]
        halo_out[q, 128:256, :] = parts[pair_ref[2 * q + 1]]
        tag0 = block_ref[2 * q].astype(F32)
        tag1 = block_ref[2 * q + 1].astype(F32)
        halo_out[q, 256:272, :] = jnp.where(tag_row == 0, tag0, tag1).astype(BF16)
        return carry

    lax.fori_loop(0, 16, fill, 0)
    met()
    pltpu.make_async_copy(halo_out.at[dom], halo_in.at[dom], swap_sem.at[2]).start()
    for k in range(1, 16):
        to = lax.rem(dom + k, 16)
        pltpu.make_async_remote_copy(
            halo_out.at[to],
            halo_in.at[dom],
            swap_sem.at[0],
            swap_sem.at[1],
            device_id=(table, to),
            device_id_type=MESH,
        ).start()
    place = slot_t_ref[...]
    for p in range(32):
        select[p * 128 : (p + 1) * 128, :] = jnp.where(place == float(p), 1.0, 0.0).astype(BF16)
    swap_wait(halo_out, halo_in, swap_sem.at[0], swap_sem.at[1], swap_sem.at[2], 15)

    def collect(c, carry):
        total = d_self[c]
        here = c.astype(F32)
        for q in range(16):
            tags = halo_in[q, 256:272, :].astype(F32)
            for s in range(2):
                piece = halo_in[q, s * 128 : (s + 1) * 128, :].astype(F32)
                total = total + jnp.where(tags[s : s + 1, :] == here, piece, 0.0)
        d_self[c] = total
        return carry

    lax.fori_loop(0, 4, collect, 0)
    d_feature = d_self[...].reshape(512, 128).astype(BF16)

    def spread(g, carry):
        rows = dot(select[pl.ds(pl.multiple_of(g * 1024, 1024), 1024), :], d_feature)
        for q in range(8):
            wide[pl.ds(g * 8 + q, 128, stride=32), :] = rows[q * 128 : (q + 1) * 128, :]
        return carry

    lax.fori_loop(0, 4, spread, 0)
    out_rows[...] = wide[...].reshape(128, 32, 128).astype(BF16)
    swap_start(out_rows, in_rows, swap_sem.at[3], swap_sem.at[4], swap_sem.at[5])
    swap_wait(out_rows, in_rows, swap_sem.at[3], swap_sem.at[4], swap_sem.at[5])


def scatter_kernel(asked_ref, rows_ref, grad_ref, low_b, wide, ordered, onehot, terms):
    c2 = pl.program_id(0)

    @pl.when(c2 == 0)
    def _():
        asked = asked_ref[...].reshape(128, 128)
        high, low = rows_asked(asked)
        for p in range(32):
            low_b[p] = jnp.broadcast_to(low[:, p : p + 1], (128, 128))
        high_t = high.T
        for p in range(32):
            onehot[:, p * 128 : (p + 1) * 128] = jnp.where(
                iota((1024, 128), 0) == high_t[p : p + 1, :], 1.0, 0.0
            ).astype(BF16)
        wide[...] = rows_ref[...].astype(F32).reshape(4096, 128)
        for p in range(32):
            ordered[p] = wide[pl.ds(p, 128, stride=32), :]

    for p in range(32):
        for c in range(2):
            terms[p * 128 : (p + 1) * 128, c * 128 : (c + 1) * 128] = jnp.where(
                low_b[p] == c2 * 2 + c, ordered[p], 0.0
            ).astype(BF16)
    total = dot(onehot[...], terms[...])
    grad_ref[0:1024, :] = total[:, 0:128]
    grad_ref[1024:2048, :] = total[:, 128:256]


def whole(count):
    return [pl.BlockSpec(memory_space=pltpu.VMEM)] * count


def body(
    tables,
    owner_ids,
    row_ids,
    neighbour_part,
    neighbour_block,
    adjacency,
    w_in,
    w_pool,
    w_self,
    w_neigh,
    out_gain,
    cotangent,
):
    shape = jax.ShapeDtypeStruct
    vmem = pltpu.VMEM
    key = owner_ids * 8192 + row_ids
    fa, asked, slot_t, wip, wis = pl.pallas_call(
        front_kernel,
        name="front",
        out_shape=(
            shape((64, 128, 128), BF16),
            shape((128, 1, 128), F32),
            shape((128, 512), F32),
            shape((256, 1024), BF16),
            shape((256, 1024), BF16),
        ),
        in_specs=whole(2) + [pl.BlockSpec(memory_space=pl.ANY)] + whole(3),
        out_specs=tuple(whole(5)),
        scratch_shapes=[
            vmem((8192, 128), F32),
            vmem((1024, 1024), BF16),
            vmem((128, 1, 128), F32),
            vmem((512, 128), F32),
            vmem((4096, 128), F32),
            vmem((128, 32, 128), BF16),
            vmem((128, 32, 128), BF16),
            vmem((1024, 1024), BF16),
            vmem((32, 128, 128), jnp.int32),
            vmem((32, 128, 128), jnp.int32),
            vmem((512, 4096), BF16),
            vmem((4096, 128), BF16),
            pltpu.SemaphoreType.DMA,
            pltpu.SemaphoreType.DMA((6,)),
            pltpu.SemaphoreType.DMA((2, 20)),
            pltpu.SemaphoreType.DMA((2, 20)),
        ],
        compiler_params=pltpu.CompilerParams(
            collective_id=0, has_side_effects=True, vmem_limit_bytes=LIMIT
        ),
    )(key, key.T, tables[0], w_in, w_pool, w_self)

    part = neighbour_part.reshape(16)
    block = neighbour_block.reshape(16)
    number = jnp.arange(16, dtype=jnp.int32)
    rank = jnp.sum((part[:, None] == part[None, :]) & (number[None, :] < number[:, None]), axis=1)
    named = (2 * part + rank)[None, :] == jnp.arange(32, dtype=jnp.int32)[:, None]
    pair = jnp.sum(jnp.where(named, number[None, :], 0), axis=1)
    tag = jnp.sum(jnp.where(named, block[None, :] + 1, 0), axis=1) - 1
    node_out, rows = pl.pallas_call(
        back_kernel,
        name="back",
        out_shape=(shape((512, 1024), BF16), shape((128, 32, 128), BF16)),
        in_specs=[pl.BlockSpec(memory_space=pltpu.SMEM)] * 3 + whole(8),
        out_specs=tuple(whole(2)),
        scratch_shapes=[
            vmem((512, 256), BF16),
            vmem((512, 1024), BF16),
            vmem((4, 512, 1024), F32),
            vmem((4, 128, 128), F32),
            vmem((4, 128, 1024), BF16),
            vmem((512, 1024), F32),
            vmem((512, 1024), BF16),
            vmem((4, 128, 1024), BF16),
            vmem((4, 128, 128), F32),
            vmem((16, 128, 128), BF16),
            vmem((16, 272, 128), BF16),
            vmem((16, 272, 128), BF16),
            vmem((4096, 512), BF16),
            vmem((4096, 128), F32),
            vmem((128, 32, 128), BF16),
            pltpu.SemaphoreType.DMA((6,)),
        ],
        compiler_params=pltpu.CompilerParams(
            collective_id=1, has_side_effects=True, vmem_limit_bytes=LIMIT
        ),
    )(
        part * 4 + block,
        pair,
        tag,
        fa,
        slot_t,
        wip,
        wis,
        w_neigh,
        out_gain.reshape(1, 1024),
        adjacency,
        cotangent,
    )
    table_grad = pl.pallas_call(
        scatter_kernel,
        name="scatter",
        grid=(4,),
        out_shape=shape((8192, 128), F32),
        in_specs=whole(2),
        out_specs=pl.BlockSpec((2048, 128), lambda c: (c, 0)),
        scratch_shapes=[
            vmem((32, 128, 128), jnp.int32),
            vmem((4096, 128), F32),
            vmem((32, 128, 128), F32),
            vmem((1024, 4096), BF16),
            vmem((4096, 256), BF16),
        ],
        compiler_params=pltpu.CompilerParams(vmem_limit_bytes=LIMIT),
    )(asked, rows)
    return (node_out, table_grad[None])


def solution(mesh):
    rows = P(("table", "dom"), None)
    placed = (
        P("table", "dom", None),
        rows,
        rows,
        rows,
        rows,
        P(("table", "dom"), None, None, None),
        P(),
        P(),
        P(),
        P(),
        P(),
        rows,
    )
    return jax.shard_map(
        body,
        mesh=mesh,
        in_specs=placed,
        out_specs=(rows, P("table", "dom", None)),
        check_vma=False,
    )
```

time: 501 us -> 149 us (0.30)
  waiting for transfers between devices: 253 us -> 0 us
  Pallas kernels: 0 us -> 141 us
  other arithmetic: 84.3 us -> 2.59 us
  local copies, waits for them, and re-layouts: 75.8 us -> 4.64 us
  matrix products: 29.2 us -> 0 us
  starting transfers between devices: 22.4 us -> 0 us
  blocking collectives: 21.1 us -> 0 us
  between operations: 14.4 us -> 0.66 us
    all_to_all x4 -> x0, waiting for transfers between devices: 156 us -> none  [the longest x1 118 us: body(): lax.all_to_all(outgoing.reshape(domains, halo_cap, block_rows, hidden_wid...]
    pallas_call x0 -> x3, Pallas kernels: none -> 141 us  [the longest x1 66.2 us: body(): pl.pallas_call(front_kernel, name='front', out_shape=(shape((64, 128, 128...]
    all_gather x1 -> x0, waiting for transfers between devices: 96.6 us -> none  [body(): gathered = lax.all_gather(pooled, 'dom', axis=0, tiled=True)]
    scatter-add x2 -> x0, other arithmetic: 57.6 us -> none  [the longest x1 33 us: body(): d_pooled = jnp.zeros((block_count, block_rows, hidden_width), jnp.float32...]
    dot_general x9 -> x0, matrix products: 29.2 us -> none  [the longest x3 10.1 us: times_transpose(): lax.dot_general(left_side, right_side, (((1,), (1,)), ((), ())), preferre...]
    gather x3 -> x0, local copies, waits for them, and re-layouts: 28.9 us -> none  [the longest x1 13.2 us: body(): fetched = jnp.where(present[:, :, None], tables[0][safe_rows], 0.0)]
    scatter x4 -> x0, local copies, waits for them, and re-layouts: 26.5 us -> none  [the longest x1 10.9 us: body(): outgoing = jnp.zeros((domains * halo_cap, block_rows, hidden_width), jnp....]
    convert_element_type x8 -> x0, other arithmetic: 23.1 us -> none  [the longest x1 11.3 us: body(): back_grads.reshape(domains * halo_cap, block_rows, hidden_width)]
  transfers between devices with their start and end apart: 5 -> 0, of which waited for: 4 -> 0; matrix products, arithmetic and copies ran while one was open for 12% -> 0% of each run, Pallas kernels for 0% -> 0%
where the time goes in v1:
time: 149 us
  Pallas kernels  141 us (95%)
  local copies, waits for them, and re-layouts  4.64 us (3%)
  other arithmetic  2.59 us (2%)
    pallas_call x1, Pallas kernels, body(): pl.pallas_call(front_kernel, name='front', out_shape=(shape((64, 128, 128...  66.2 us
    pallas_call x1, Pallas kernels, body(): pl.pallas_call(back_kernel, name='back', out_shape=(shape((512, 1024), BF...  55 us
    pallas_call x1, Pallas kernels, body(): pl.pallas_call(scatter_kernel, name='scatter', grid=(4,), out_shape=shape...  19.9 us

profile of v1, /device:TPU:1, one launch (start us, length us, event | category | flops | bytes accessed | tf_op | source)
XLA Modules:
  0.0 149.0 jit_solution(15189396590978477140)
XLA Ops:
  0.6 0.8 reshape.30
  1.4 0.2 convert_reduce_fusion
  1.6 0.8 reshape.31
  2.3 0.5 multiply_add_fusion.1
  2.9 0.7 select_reduce_fusion
  3.5 0.5 broadcast_add_fusion.block_ref
  4.0 1.3 reshape.32.gain_ref
  5.3 0.7 multiply_add_fusion
  6.0 0.0 copy-start.1
  6.0 0.9 copy.15.key_ref
  6.9 0.0 copy-done.1
  6.9 66.2 %front.1 = (bf16[64,128,128]{2,1,0:T(8,128)(2,1)}, f32[128,1,128]{2,1,0:T(1,128)}, f32[128,512]{1,0:T(8,128)}, bf16[256,1024]{1,0:T(8,128)(2,1)}, bf16[256,1024]{1,0:T(8,128)(2,1)}) custom-call(s32[512,4]{1,0:T(8,128)} %copy.15.key_ref, s32[4,512]{1,0:T(4,128)} %bitcast.5, f32[8192,128]{1,0:T(8,128)} %bitcast.3, bf16[128,1024]{1,0:T(8,128)(2,1)} %w_in_ref.1, ...), custom_call_target="tpu_custom_call" | custom-call | tf_op jit(solution)/shard_map/front/pallas_call | solution.py:467
  73.1 55.0 %back.1 = (bf16[512,1024]{1,0:T(8,128)(2,1)}, bf16[128,32,128]{2,1,0:T(8,128)(2,1)}) custom-call(s32[16]{0:T(128)} %get-tuple-element.19.source_ref, s32[32]{0:T(128)} %get-tuple-element.17.pair_ref, s32[32]{0:T(128)} %broadcast_add_fusion.block_ref, bf16[64,128,128]{2,1,0:T(8,128)(2,1)} %get-tuple-element.9.fa_ref, ...), custom_call_target="tpu_custom_call" | custom-call | tf_op jit(solution)/shard_map/back/pallas_call | solution.py:509
  128.1 0.0 copy-start
  128.1 19.9 %scatter.1 = f32[8192,128]{1,0:T(8,128)} custom-call(f32[128,1,128]{2,1,0:T(1,128)} %get-tuple-element.14.asked_ref, bf16[128,32,128]{2,1,0:T(8,128)(2,1)} %get-tuple-element.15.rows_ref), custom_call_target="tpu_custom_call" | custom-call | tf_op jit(solution)/shard_map/scatter/pallas_call | solution.py:549
  148.0 0.0 copy-done
  148.0 1.0 copy.17
Async XLA Ops:
  6.0 0.9 copy-start.1
  128.1 19.9 %copy-start = (bf16[512,1024]{1,0:T(8,128)(2,1)S(1)}, bf16[512,1024]{1,0:T(8,128)(2,1)}, u32[]{:S(2)}) copy-start(bf16[512,1024]{1,0:T(8,128)(2,1)} %get-tuple-element.23) | copy-start | bytes 3145732

commit v2 on v1

v2 whole, which is shorter than its diff:
```python
import jax
import jax.numpy as jnp
from jax import lax
from jax.experimental import pallas as pl
from jax.experimental.pallas import tpu as pltpu
from jax.sharding import PartitionSpec as P

EPSILON = 1e-06
MESH = pl.DeviceIdType.MESH
F32 = jnp.float32
BF16 = jnp.bfloat16
LIMIT = 62 * 1024 * 1024
NT = ((1,), (1,))


def iota(shape, dim):
    return lax.broadcasted_iota(jnp.int32, shape, dim)


def dot(a, b, dims=((1,), (0,))):
    return lax.dot_general(a, b, (dims, ((), ())), preferred_element_type=F32)


def each_of_table(step, act):
    there = lax.rem(lax.axis_index("table") + step, 8)
    dom = lax.axis_index("dom")

    def body(k, carry):
        act(there, lax.rem(dom + k, 16))
        return carry

    first = jnp.where(step == 0, 1, 0) if not isinstance(step, int) else int(step == 0)
    lax.fori_loop(first, 16, body, 0)


def greet():
    barrier = pltpu.get_barrier_semaphore()
    for step in range(8):
        each_of_table(
            step,
            lambda t, d: pl.semaphore_signal(barrier, inc=1, device_id=(t, d), device_id_type=MESH),
        )


def met():
    pl.semaphore_wait(pltpu.get_barrier_semaphore(), 127)


def send_table(step, out_ref, in_ref, send, recv):
    me = lax.axis_index("table") * 16 + lax.axis_index("dom")
    each_of_table(
        step,
        lambda t, d: pltpu.make_async_remote_copy(
            out_ref.at[t * 16 + d], in_ref.at[me], send, recv, device_id=(t, d), device_id_type=MESH
        ).start(),
    )


def all_of(count, out_ref, in_ref, send, recv):
    return pltpu.make_async_remote_copy(
        out_ref.at[pl.ds(0, count)],
        in_ref.at[pl.ds(0, count)],
        send,
        recv,
        device_id=(lax.axis_index("table"), lax.rem(lax.axis_index("dom") + 1, 16)),
        device_id_type=MESH,
    )


def send_requests(request, asked, send, recv):
    for step in range(8):
        send_table(step, request, asked, send, recv)


def send_halo(halo_out, halo_in, send, recv):
    table, dom = lax.axis_index("table"), lax.axis_index("dom")
    for k in range(1, 16):
        to = lax.rem(dom + k, 16)
        pltpu.make_async_remote_copy(
            halo_out.at[to], halo_in.at[dom], send, recv, device_id=(table, to), device_id_type=MESH
        ).start()


def wait_send(*args):
    all_of(*args).wait_send()


def wait_recv(*args):
    all_of(*args).wait_recv()


def gather_group(fa_ref, send, recv, meanwhile):
    table, dom = lax.axis_index("table"), lax.axis_index("dom")
    z, x = dom // 4, lax.rem(dom, 4)

    def place(h, i, j):
        dz, dx = (j, i) if h == 0 else (i, j)
        return lax.rem(z + dz + 4, 4) * 4 + lax.rem(x + dx + 4, 4)

    def copy(h, number, piece, start, count, to):
        blocks = fa_ref.at[pl.ds(place(h, *piece) * 4 + 2 * h + start, count)]
        return pltpu.make_async_remote_copy(
            blocks,
            blocks,
            send.at[h, number],
            recv.at[h, number],
            device_id=(table, place(h, *to)),
            device_id_type=MESH,
        )

    up, down = (1, 0), (-1, 0)
    away, back = (0, 1), (0, -1)
    pieces = (0, -1, 1, 2)
    first = (up, down)
    across = (away, back)
    sides = (0, 1)

    def near(h, side):
        return copy(h, side, (0, 0), 0, 2, first[side])

    def far(h, side):
        return copy(h, 2 + side, (2 * side - 1, 0), side, 1, first[side])

    def second(h, n, side):
        return copy(h, 4 + 4 * n + side, (pieces[n], 0), 0, 2, across[side])

    def second_far(h, n, side):
        return copy(h, 6 + 4 * n + side, (pieces[n], 2 * side - 1), side, 1, across[side])

    def near_in(h, side):
        return copy(h, side, (2 * side - 1, 0), 0, 2, first[side])

    def far_in(h, side):
        return copy(h, 2 + side, (2, 0), side, 1, first[side])

    def second_in(h, n, side):
        return copy(h, 4 + 4 * n + side, (pieces[n], 2 * side - 1), 0, 2, across[side])

    def second_far_in(h, n, side):
        return copy(h, 6 + 4 * n + side, (pieces[n], 2), side, 1, across[side])

    for h in range(2):
        for side in sides:
            near(h, side).start()
    for h in range(2):
        for side in sides:
            second(h, 0, side).start()
    meanwhile()
    for side in sides:
        for h in range(2):
            near_in(h, side).wait_recv()
            far(h, side).start()
            for other in sides:
                second(h, 1 + side, other).start()
    for side in sides:
        for h in range(2):
            second_in(h, 0, side).wait_recv()
            second_far(h, 0, side).start()
    for h in range(2):
        for side in sides:
            far_in(h, side).wait_recv()
        for side in sides:
            second(h, 3, side).start()
    for n in (1, 2, 3):
        for side in sides:
            for h in range(2):
                second_in(h, n, side).wait_recv()
                second_far(h, n, side).start()
    for h in range(2):
        for side in sides:
            near(h, side).wait_send()
            far(h, side).wait_send()
            for n in range(4):
                second_far_in(h, n, side).wait_recv()
                second(h, n, side).wait_send()
                second_far(h, n, side).wait_send()


def two_part(w_ref, product):
    high = product.astype(BF16)
    w_ref[0:128, :] = high
    w_ref[128:256, :] = (product - high.astype(F32)).astype(BF16)


def step_kernel(
    owner_ref,
    row_ref,
    part_ref,
    block_ref,
    w_in_ref,
    gain_ref,
    tables_hbm,
    w_pool_hbm,
    w_self_hbm,
    w_neigh_hbm,
    adjacency_hbm,
    cotangent_hbm,
    node_out_hbm,
    grad_hbm,
    table,
    w_pool,
    w_self,
    w_neigh,
    adjacency,
    cotangent,
    node_out,
    packed,
    request,
    asked,
    slot,
    row_b,
    out_rows,
    in_rows,
    in_grads,
    onehot,
    select,
    fa,
    wip,
    wis,
    stacked,
    pooled,
    slope,
    inverse,
    mean,
    pre_act,
    d_pre,
    d_scaled,
    d_self,
    parts,
    halo_out,
    halo_in,
    rows_hot,
    terms,
    load_sem,
    one_sem,
    rows_send,
    rows_recv,
    grads_send,
    grads_recv,
    ring_send,
    ring_recv,
    grad_sem,
):
    table_id, dom = lax.axis_index("table"), lax.axis_index("dom")
    me = table_id * 16 + dom
    greet()
    loads = [
        pltpu.make_async_copy(source, target, load_sem.at[i])
        for i, (source, target) in enumerate(
            (
                (tables_hbm, table),
                (w_pool_hbm, w_pool),
                (w_self_hbm, w_self),
                (w_neigh_hbm, w_neigh),
                (adjacency_hbm, adjacency),
                (cotangent_hbm, cotangent),
            )
        )
    ]
    for load in loads:
        load.start()

    subs = iota((128, 512), 0)
    place32 = lax.rem(subs, 32)
    hits = [jnp.where(owner_ref[j : j + 1, :] == subs, 1.0, 0.0) for j in range(4)]
    hit = sum(hits)
    before = jnp.where(iota((512, 512), 0) < iota((512, 512), 1), 1.0, 0.0).astype(BF16)
    rank = dot(hit.astype(BF16), before)
    slot[...] = jnp.where(hit > 0.5, rank, -1.0)
    above = jnp.zeros((128, 128), F32)
    below = jnp.zeros((128, 128), F32)
    for j in range(4):
        position = jnp.sum(hits[j] * rank, axis=0, keepdims=True).astype(jnp.int32)
        row = row_ref[j : j + 1, :]
        row_a = row >> 7
        row_c = (row - row_a * 128).astype(F32)
        row_a = (row_a + 1).astype(F32)
        here = place32 == position
        hot = hits[j].astype(BF16)
        above = above + dot(hot, jnp.where(here, row_a, 0.0).astype(BF16), NT)
        below = below + dot(hot, jnp.where(here, row_c, 0.0).astype(BF16), NT)
    asks = jnp.where(above > 0.5, (above - 1.0) * 128.0 + below, -1.0).astype(jnp.int32)
    request[...] = asks.reshape(128, 1, 128)
    asked[pl.ds(me, 1)] = request[pl.ds(me, 1)]
    met()
    send_requests(request, asked, one_sem.at[0], one_sem.at[1])
    loads[0].wait()
    for c in range(8):
        packed[:, c * 128 : (c + 1) * 128] = table[c * 1024 : (c + 1) * 1024, :].astype(BF16)
    loads[1].wait()
    two_part(wip, dot(w_in_ref[...], w_pool[...]))
    loads[2].wait()
    two_part(wis, dot(w_in_ref[...], w_self[...]))
    wait_recv(127, request, asked, one_sem.at[0], one_sem.at[1])

    asked_t = asked[...].reshape(128, 128).astype(F32).T.astype(jnp.int32)
    for o in range(128):
        row_b[o * 32 : (o + 1) * 32, :] = jnp.broadcast_to(asked_t[0:32, o : o + 1], (32, 128))
    lane = iota((64, 128), 1)

    def lookup(g, carry):
        there = [lax.rem(table_id + 2 * g + i, 8) for i in range(2)]
        for i in range(2):
            for r in range(8):
                start = pl.multiple_of(there[i] * 512 + r * 64, 64)
                high = row_b[pl.ds(start, 64), :] & 1023
                low = i * 512 + r * 64
                for c in range(8):
                    onehot[low : low + 64, c * 128 : (c + 1) * 128] = jnp.where(
                        high == lane + c * 128, 1.0, 0.0
                    ).astype(BF16)
        found = dot(onehot[...], packed[...])
        for i in range(2):
            for r in range(8):
                start = pl.multiple_of(there[i] * 512 + r * 64, 64)
                chunk = row_b[pl.ds(start, 64), :] >> 10
                low = i * 512 + r * 64
                total = jnp.zeros((64, 128), F32)
                for c in range(8):
                    total = total + jnp.where(
                        chunk == c, found[low : low + 64, c * 128 : (c + 1) * 128], 0.0
                    )
                out_rows[pl.ds(there[i] * 16 + r * 2, 2)] = total.astype(BF16).reshape(2, 32, 128)
            send_table(2 * g + i, out_rows, in_rows, rows_send, rows_recv.at[g])
        return carry

    lax.fori_loop(0, 4, lookup, 0)
    in_rows[pl.ds(me, 1)] = out_rows[pl.ds(me, 1)]
    wait_send(127, request, asked, one_sem.at[0], one_sem.at[1])
    sub32 = iota((32, 512), 0).astype(F32)
    for o in range(128):
        select[o * 32 : (o + 1) * 32, :] = jnp.where(slot[o : o + 1, :] == sub32, 1.0, 0.0).astype(
            BF16
        )
    feature_t = jnp.zeros((128, 512), F32)
    for g in range(4):
        wait_recv(31 if g == 0 else 32, out_rows, in_rows, rows_send, rows_recv.at[g])
        for i in range(2):
            there = lax.rem(table_id - 2 * g - i + 8, 8)
            got = in_rows[pl.ds(there * 16, 16)].reshape(512, 128)
            feature_t = feature_t + dot(
                got.T, select[pl.ds(pl.multiple_of(there * 512, 512), 512), :]
            )
    feature = feature_t.T.astype(BF16)
    fa[pl.ds(dom * 4, 4)] = feature.reshape(4, 128, 128)
    stacked[:, 0:128] = feature
    stacked[:, 128:256] = feature

    def meanwhile():
        pre_act[...] = dot(stacked[...], wis[...])
        wait_send(127, out_rows, in_rows, rows_send, rows_recv.at[0])
        for load in loads[3:]:
            load.wait()

    gather_group(fa, ring_send, ring_recv, meanwhile)

    def forward(b, carry):
        for k in range(4):
            f = fa[part_ref[b, k] * 4 + block_ref[b, k]]
            stacked[k * 128 : (k + 1) * 128, 0:128] = f
            stacked[k * 128 : (k + 1) * 128, 128:256] = f
        pre = dot(stacked[...], wip[...])
        s = jax.nn.sigmoid(pre)
        pooled[...] = (pre * s).astype(BF16)
        slope[b] = s * (1.0 + pre * (1.0 - s))
        edges = jnp.concatenate([adjacency[b, k] for k in range(4)], axis=1)
        inv = 1.0 / jnp.sum(edges.astype(F32), axis=1, keepdims=True)
        inverse[b] = jnp.broadcast_to(inv, (128, 128))
        mean[b] = (dot(edges, pooled[...]) * inv).astype(BF16)
        return carry

    lax.fori_loop(0, 4, forward, 0)
    pre_act[...] += dot(mean[...].reshape(512, 1024), w_neigh[...])
    gain = gain_ref[...].astype(F32).reshape(1, 1024)

    def norm(r, carry):
        rows = pl.ds(pl.multiple_of(r * 32, 32), 32)
        pre = pre_act[rows, :]
        s = jax.nn.sigmoid(pre)
        active = pre * s
        rms = lax.rsqrt(jnp.mean(active * active, axis=1, keepdims=True) + EPSILON)
        node_out[rows, :] = (active * rms * gain).astype(BF16)
        weighted = gain * cotangent[rows, :].astype(F32)
        d_active = rms * weighted - active * (rms * rms * rms) * jnp.mean(
            weighted * active, axis=1, keepdims=True
        )
        d_pre[rows, :] = (d_active * (s * (1.0 + pre * (1.0 - s)))).astype(BF16)
        return carry

    lax.fori_loop(0, 16, norm, 0)
    store = pltpu.make_async_copy(node_out, node_out_hbm, load_sem.at[6])
    store.start()
    d_mean = dot(d_pre[...], w_neigh[...], NT)
    for b in range(4):
        d_scaled[b] = (d_mean[b * 128 : (b + 1) * 128, :] * inverse[b][:, 0:1]).astype(BF16)
    both = dot(d_pre[...], wis[...], NT)
    d_self[...] = (both[:, 0:128] + both[:, 128:256]).reshape(4, 128, 128)

    def backward(b, carry):
        edges = jnp.concatenate([adjacency[b, k].T for k in range(4)], axis=0)
        d_pool = dot(edges, d_scaled[b]) * slope[b]
        pair = dot(d_pool.astype(BF16), wip[...], NT)
        parts[pl.ds(b * 4, 4)] = (
            (pair[:, 0:128] + pair[:, 128:256]).astype(BF16).reshape(4, 128, 128)
        )
        return carry

    lax.fori_loop(0, 4, backward, 0)
    tag_row = iota((16, 128), 0)

    def fill(q, carry):
        count = jnp.int32(0)
        pairs = [jnp.int32(0), jnp.int32(0)]
        tags = [jnp.int32(-1), jnp.int32(-1)]
        for i in range(16):
            named = part_ref[i // 4, i % 4] == q
            for s in range(2):
                taken = named & (count == s)
                pairs[s] = jnp.where(taken, i, pairs[s])
                tags[s] = jnp.where(taken, block_ref[i // 4, i % 4], tags[s])
            count = count + jnp.where(named, 1, 0)
        halo_out[q, 0:128, :] = parts[pairs[0]]
        halo_out[q, 128:256, :] = parts[pairs[1]]
        halo_out[q, 256:272, :] = jnp.where(
            tag_row == 0, tags[0].astype(F32), tags[1].astype(F32)
        ).astype(BF16)
        return carry

    lax.fori_loop(0, 16, fill, 0)
    halo_in[pl.ds(dom, 1)] = halo_out[pl.ds(dom, 1)]
    send_halo(halo_out, halo_in, one_sem.at[2], one_sem.at[3])
    lane4 = iota((1, 128), 1) >> 5
    tall = iota((1024, 128), 0)

    def heat(t, carry):
        names = asked[pl.ds(t * 16, 16)].reshape(16, 128) & 1023
        for i in range(4):
            mixed = names[4 * i : 4 * i + 1, :]
            for k in range(1, 4):
                mixed = jnp.where(lane4 == k, names[4 * i + k : 4 * i + k + 1, :], mixed)
            rows_hot[t, :, i * 128 : (i + 1) * 128] = jnp.where(tall == mixed, 1.0, 0.0).astype(
                BF16
            )
        return carry

    lax.fori_loop(0, 8, heat, 0)
    wait_recv(15, halo_out, halo_in, one_sem.at[2], one_sem.at[3])

    def collect(c, carry):
        total = d_self[c]
        here = c.astype(F32)
        for q in range(16):
            tags = halo_in[q, 256:272, :].astype(F32)
            for s in range(2):
                piece = halo_in[q, s * 128 : (s + 1) * 128, :].astype(F32)
                total = total + jnp.where(tags[s : s + 1, :] == here, piece, 0.0)
        d_self[c] = total
        return carry

    lax.fori_loop(0, 4, collect, 0)
    d_feature = d_self[...].reshape(512, 128).astype(BF16)

    def spread(step, carry):
        there = lax.rem(table_id + step, 8)
        rows = dot(select[pl.ds(pl.multiple_of(there * 512, 512), 512), :], d_feature)
        out_rows[pl.ds(there * 16, 16)] = rows.astype(BF16).reshape(16, 32, 128)
        send_table(step, out_rows, in_grads, grads_send, grads_recv.at[step // 2])
        return carry

    lax.fori_loop(0, 8, spread, 0)
    in_grads[pl.ds(me, 1)] = out_rows[pl.ds(me, 1)]
    wait_send(15, halo_out, halo_in, one_sem.at[2], one_sem.at[3])

    for g in range(4):
        wait_recv(31 if g == 0 else 32, out_rows, in_grads, grads_send, grads_recv.at[g])
        there = [lax.rem(table_id - 2 * g - i + 8, 8) for i in range(2)]
        for i in range(2):
            onehot[:, i * 512 : (i + 1) * 512] = rows_hot[there[i]]

        def add(c2, carry):
            for i in range(2):
                for r in range(8):
                    start = pl.multiple_of(there[i] * 512 + r * 64, 64)
                    chunk = row_b[pl.ds(start, 64), :] >> 10
                    low = i * 512 + r * 64
                    rows = (
                        in_grads[pl.ds(there[i] * 16 + r * 2, 2)].reshape(64, 128).astype(F32)
                    )
                    for c in range(2):
                        terms[low : low + 64, c * 128 : (c + 1) * 128] = jnp.where(
                            chunk == c2 * 2 + c, rows, 0.0
                        ).astype(BF16)
            total = dot(onehot[...], terms[...])
            for c in range(2):
                rows = pl.ds(pl.multiple_of((c2 * 2 + c) * 1024, 1024), 1024)
                if g == 0:
                    table[rows, :] = total[:, c * 128 : (c + 1) * 128]
                else:
                    table[rows, :] += total[:, c * 128 : (c + 1) * 128]
            if g == 3:
                rows = pl.ds(pl.multiple_of(c2 * 2048, 2048), 2048)
                pltpu.make_async_copy(table.at[rows], grad_hbm.at[rows], grad_sem.at[c2]).start()
            return carry

        lax.fori_loop(0, 4, add, 0)
    wait_send(127, out_rows, in_grads, grads_send, grads_recv.at[0])
    store.wait()
    for c2 in range(4):
        rows = pl.ds(c2 * 2048, 2048)
        pltpu.make_async_copy(table.at[rows], grad_hbm.at[rows], grad_sem.at[c2]).wait()


def body(
    tables,
    owner_ids,
    row_ids,
    neighbour_part,
    neighbour_block,
    adjacency,
    w_in,
    w_pool,
    w_self,
    w_neigh,
    out_gain,
    cotangent,
):
    shape = jax.ShapeDtypeStruct
    vmem = pltpu.VMEM
    dma = pltpu.SemaphoreType.DMA
    held = [pl.BlockSpec(memory_space=pltpu.VMEM)]
    scalar = [pl.BlockSpec(memory_space=pltpu.SMEM)]
    anywhere = [pl.BlockSpec(memory_space=pl.ANY)]
    node_out, table_grad = pl.pallas_call(
        step_kernel,
        name="step",
        out_shape=(shape((512, 1024), BF16), shape((8192, 128), F32)),
        in_specs=held * 2 + scalar * 2 + held * 2 + anywhere * 6,
        out_specs=tuple(anywhere * 2),
        scratch_shapes=[
            vmem((8192, 128), F32),
            vmem((1024, 1024), BF16),
            vmem((1024, 1024), BF16),
            vmem((1024, 1024), BF16),
            vmem((4, 4, 128, 128), BF16),
            vmem((512, 1024), BF16),
            vmem((512, 1024), BF16),
            vmem((1024, 1024), BF16),
            vmem((128, 1, 128), jnp.int32),
            vmem((128, 1, 128), jnp.int32),
            vmem((128, 512), F32),
            vmem((4096, 128), jnp.int32),
            vmem((128, 32, 128), BF16),
            vmem((128, 32, 128), BF16),
            vmem((128, 32, 128), BF16),
            vmem((1024, 1024), BF16),
            vmem((4096, 512), BF16),
            vmem((64, 128, 128), BF16),
            vmem((256, 1024), BF16),
            vmem((256, 1024), BF16),
            vmem((512, 256), BF16),
            vmem((512, 1024), BF16),
            vmem((4, 512, 1024), F32),
            vmem((4, 128, 128), F32),
            vmem((4, 128, 1024), BF16),
            vmem((512, 1024), F32),
            vmem((512, 1024), BF16),
            vmem((4, 128, 1024), BF16),
            vmem((4, 128, 128), F32),
            vmem((16, 128, 128), BF16),
            vmem((16, 272, 128), BF16),
            vmem((16, 272, 128), BF16),
            vmem((8, 1024, 512), BF16),
            vmem((1024, 256), BF16),
            dma((7,)),
            dma((4,)),
            dma,
            dma((4,)),
            dma,
            dma((4,)),
            dma((2, 20)),
            dma((2, 20)),
            dma((4,)),
        ],
        compiler_params=pltpu.CompilerParams(
            collective_id=0, has_side_effects=True, vmem_limit_bytes=LIMIT
        ),
    )(
        owner_ids.T,
        row_ids.T,
        neighbour_part,
        neighbour_block,
        w_in,
        out_gain,
        tables[0],
        w_pool,
        w_self,
        w_neigh,
        adjacency,
        cotangent,
    )
    return (node_out, table_grad[None])


def solution(mesh):
    rows = P(("table", "dom"), None)
    placed = (
        P("table", "dom", None),
        rows,
        rows,
        rows,
        rows,
        P(("table", "dom"), None, None, None),
        P(),
        P(),
        P(),
        P(),
        P(),
        rows,
    )
    return jax.shard_map(
        body,
        mesh=mesh,
        in_specs=placed,
        out_specs=(rows, P("table", "dom", None)),
        check_vma=False,
    )
```

time: 149 us -> 125 us (0.84)
  the two profiles are of different devices: /device:TPU:1 before, /device:TPU:13 now
where the time goes in v2:
time: 125 us
  Pallas kernels  118 us (94%)
  local copies, waits for them, and re-layouts  6.73 us (5%)
    pallas_call x1, Pallas kernels, body(): pl.pallas_call(step_kernel, name='step', out_shape=(shape((512, 1024), BF...  118 us
    unnamed x2, local copies, waits for them, and re-layouts  6.73 us

profile of v2, /device:TPU:13, one launch (start us, length us, event | category | flops | bytes accessed | tf_op | source)
XLA Modules:
  0.0 125.2 jit_solution(17182145398824577233)
XLA Ops:
  0.6 117.8 %step.1 = (bf16[512,1024]{1,0:T(8,128)(2,1)}, f32[8192,128]{1,0:T(8,128)}) custom-call(s32[4,512]{1,0:T(4,128)} %bitcast.6, s32[4,512]{1,0:T(4,128)} %bitcast.7, s32[4,4]{1,0:T(4,128)} %part_ref.1, s32[4,4]{1,0:T(4,128)} %block_ref.1, bf16[128,1024]{1,0:T(8,128)(2,1)} %w_in_ref.1, bf16[1024]{0:T(1024)(128)(2,1)} %gain_ref.1, f32[8192,128]{1,0:T(8,128)} %bitcast.4, ...), custom_call_target="tpu_custom_call" | custom-call | tf_op jit(solution)/shard_map/step/pallas_call | solution.py:533
  118.4 2.3 %copy.16 = bf16[512,1024]{1,0:T(8,128)(2,1)} copy(bf16[512,1024]{1,0:T(8,128)(2,1)} %get-tuple-element.8) | data formatting | bytes 2097152
  120.7 4.5 %copy.17 = f32[1,8192,128]{2,1,0:T(8,128)} copy(f32[1,8192,128]{2,1,0:T(8,128)} %bitcast.5) | data formatting | bytes 8388608

commit v3 on v2

--- a/solution.py
+++ b/solution.py
@@ -33,17 +33,21 @@
     lax.fori_loop(first, 16, body, 0)
 
 
+def peers():
+    table, dom = lax.axis_index("table"), lax.axis_index("dom")
+    return [(lax.rem(table + k, 8), dom) for k in range(1, 8)] + [
+        (table, lax.rem(dom + k, 16)) for k in range(1, 16)
+    ]
+
+
 def greet():
     barrier = pltpu.get_barrier_semaphore()
-    for step in range(8):
-        each_of_table(
-            step,
-            lambda t, d: pl.semaphore_signal(barrier, inc=1, device_id=(t, d), device_id_type=MESH),
-        )
+    for peer in peers():
+        pl.semaphore_signal(barrier, inc=1, device_id=peer, device_id_type=MESH)
 
 
 def met():
-    pl.semaphore_wait(pltpu.get_barrier_semaphore(), 127)
+    pl.semaphore_wait(pltpu.get_barrier_semaphore(), 22)
 
 
 def send_table(step, out_ref, in_ref, send, recv):
@@ -67,9 +71,66 @@
     )
 
 
-def send_requests(request, asked, send, recv):
-    for step in range(8):
-        send_table(step, request, asked, send, recv)
+def ask_tables(request, relay, send, recv):
+    table = lax.axis_index("table")
+    for peer in peers()[:7]:
+        pltpu.make_async_remote_copy(
+            request.at[peer[0]], relay.at[table], send, recv, device_id=peer, device_id_type=MESH
+        ).start()
+
+
+def ask_group(relay, asked, send, recv):
+    dom = lax.axis_index("dom")
+    for peer in peers()[7:]:
+        pltpu.make_async_remote_copy(
+            relay.at[:, peer[1]], asked.at[:, dom], send, recv, device_id=peer, device_id_type=MESH
+        ).start()
+
+
+def wait_tables(request, relay, send, recv):
+    whole = pltpu.make_async_remote_copy(
+        request.at[pl.ds(0, 7)],
+        relay.at[pl.ds(0, 7)],
+        send,
+        recv,
+        device_id=peers()[0],
+        device_id_type=MESH,
+    )
+    whole.wait_recv()
+    whole.wait_send()
+
+
+def asked_group(relay, asked, send, recv):
+    return pltpu.make_async_remote_copy(
+        relay.at[:, pl.ds(0, 15)],
+        asked.at[:, pl.ds(0, 15)],
+        send,
+        recv,
+        device_id=peers()[7],
+        device_id_type=MESH,
+    )
+
+
+def wait_group(*args):
+    asked_group(*args).wait_recv()
+
+
+def sent_group(*args):
+    asked_group(*args).wait_send()
+
+
+def pairs_of(part_ref, block_ref, q):
+    count = jnp.int32(0)
+    pairs = [jnp.int32(0), jnp.int32(0)]
+    tags = [jnp.int32(-1), jnp.int32(-1)]
+    for i in range(16):
+        named = part_ref[i // 4, i % 4] == q
+        for s in range(2):
+            taken = named & (count == s)
+            pairs[s] = jnp.where(taken, i, pairs[s])
+            tags[s] = jnp.where(taken, block_ref[i // 4, i % 4], tags[s])
+        count = count + jnp.where(named, 1, 0)
+    return pairs, tags
 
 
 def send_halo(halo_out, halo_in, send, recv):
@@ -196,7 +257,10 @@
     adjacency_hbm,
     cotangent_hbm,
     node_out_hbm,
-    grad_hbm,
+    sums_hbm,
+    hot_hbm,
+    low_hbm,
+    late_hbm,
     table,
     w_pool,
     w_self,
@@ -206,6 +270,7 @@
     node_out,
     packed,
     request,
+    relay,
     asked,
     slot,
     row_b,
@@ -280,20 +345,31 @@
         above = above + dot(hot, jnp.where(here, row_a, 0.0).astype(BF16), NT)
         below = below + dot(hot, jnp.where(here, row_c, 0.0).astype(BF16), NT)
     asks = jnp.where(above > 0.5, (above - 1.0) * 128.0 + below, -1.0).astype(jnp.int32)
-    request[...] = asks.reshape(128, 1, 128)
-    asked[pl.ds(me, 1)] = request[pl.ds(me, 1)]
+    request[...] = asks.reshape(8, 16, 1, 128)
+    relay[pl.ds(table_id, 1)] = request[pl.ds(table_id, 1)]
+
+    def tag(q, carry):
+        _, tags = pairs_of(part_ref, block_ref, q)
+        for s in range(2):
+            relay[8 + s, q] = jnp.full((1, 128), tags[s], jnp.int32)
+        return carry
+
+    lax.fori_loop(0, 16, tag, 0)
     met()
-    send_requests(request, asked, one_sem.at[0], one_sem.at[1])
+    ask_tables(request, relay, one_sem.at[0], one_sem.at[1])
     loads[0].wait()
     for c in range(8):
         packed[:, c * 128 : (c + 1) * 128] = table[c * 1024 : (c + 1) * 1024, :].astype(BF16)
+    wait_tables(request, relay, one_sem.at[0], one_sem.at[1])
+    asked[:, pl.ds(dom, 1)] = relay[:, pl.ds(dom, 1)]
+    ask_group(relay, asked, one_sem.at[4], one_sem.at[5])
     loads[1].wait()
     two_part(wip, dot(w_in_ref[...], w_pool[...]))
     loads[2].wait()
     two_part(wis, dot(w_in_ref[...], w_self[...]))
-    wait_recv(127, request, asked, one_sem.at[0], one_sem.at[1])
-
-    asked_t = asked[...].reshape(128, 128).astype(F32).T.astype(jnp.int32)
+    wait_group(relay, asked, one_sem.at[4], one_sem.at[5])
+
+    asked_t = asked[0:8].reshape(128, 128).astype(F32).T.astype(jnp.int32)
     for o in range(128):
         row_b[o * 32 : (o + 1) * 32, :] = jnp.broadcast_to(asked_t[0:32, o : o + 1], (32, 128))
     lane = iota((64, 128), 1)
@@ -326,7 +402,7 @@
 
     lax.fori_loop(0, 4, lookup, 0)
     in_rows[pl.ds(me, 1)] = out_rows[pl.ds(me, 1)]
-    wait_send(127, request, asked, one_sem.at[0], one_sem.at[1])
+    sent_group(relay, asked, one_sem.at[4], one_sem.at[5])
     sub32 = iota((32, 512), 0).astype(F32)
     for o in range(128):
         select[o * 32 : (o + 1) * 32, :] = jnp.where(slot[o : o + 1, :] == sub32, 1.0, 0.0).astype(
@@ -393,71 +469,87 @@
     d_mean = dot(d_pre[...], w_neigh[...], NT)
     for b in range(4):
         d_scaled[b] = (d_mean[b * 128 : (b + 1) * 128, :] * inverse[b][:, 0:1]).astype(BF16)
+
+    for half in range(2):
+        first = half * 64
+
+        def backward(b, carry):
+            edges = jnp.concatenate(
+                [adjacency[b, k].T[first : first + 64] for k in range(4)], axis=0
+            )
+            slopes = jnp.concatenate(
+                [slope[b, k * 128 + first : k * 128 + first + 64, :] for k in range(4)], axis=0
+            )
+            d_pool = dot(edges, d_scaled[b]) * slopes
+            pair = dot(d_pool.astype(BF16), wip[...], NT)
+            parts[pl.ds(b * 4, 4)] = (
+                (pair[:, 0:128] + pair[:, 128:256]).astype(BF16).reshape(4, 64, 128)
+            )
+            return carry
+
+        lax.fori_loop(0, 4, backward, 0)
+
+        def fill(q, carry):
+            pairs, _ = pairs_of(part_ref, block_ref, q)
+            for s in range(2):
+                halo_out[half, q, s] = parts[pairs[s]]
+            return carry
+
+        lax.fori_loop(0, 16, fill, 0)
+        halo_in[half, pl.ds(dom, 1)] = halo_out[half, pl.ds(dom, 1)]
+        send_halo(
+            halo_out.at[half], halo_in.at[half], one_sem.at[2 + 4 * half], one_sem.at[3 + 4 * half]
+        )
+    lane4 = iota((1, 128), 1) >> 5
+    tall = iota((1024, 128), 0)
+
+    def heat(g, carry):
+        for i in range(2):
+            there = lax.rem(table_id - 2 * g - i + 8, 8)
+            names = asked[there].reshape(16, 128) & 1023
+            for n in range(4):
+                mixed = names[4 * n : 4 * n + 1, :]
+                for k in range(1, 4):
+                    mixed = jnp.where(lane4 == k, names[4 * n + k : 4 * n + k + 1, :], mixed)
+                low = i * 512 + n * 128
+                rows_hot[g, :, low : low + 128] = jnp.where(tall == mixed, 1.0, 0.0).astype(BF16)
+        return carry
+
+    lax.fori_loop(0, 4, heat, 0)
+    last = [lax.rem(table_id - 6 - i + 8, 8) for i in range(2)]
+    saves = [pltpu.make_async_copy(rows_hot.at[3], hot_hbm, grad_sem.at[0])] + [
+        pltpu.make_async_copy(
+            row_b.at[pl.ds(pl.multiple_of(last[i] * 512, 512), 512)],
+            low_hbm.at[pl.ds(i * 512, 512)],
+            grad_sem.at[1 + i],
+        )
+        for i in range(2)
+    ]
+    for save in saves:
+        save.start()
     both = dot(d_pre[...], wis[...], NT)
     d_self[...] = (both[:, 0:128] + both[:, 128:256]).reshape(4, 128, 128)
-
-    def backward(b, carry):
-        edges = jnp.concatenate([adjacency[b, k].T for k in range(4)], axis=0)
-        d_pool = dot(edges, d_scaled[b]) * slope[b]
-        pair = dot(d_pool.astype(BF16), wip[...], NT)
-        parts[pl.ds(b * 4, 4)] = (
-            (pair[:, 0:128] + pair[:, 128:256]).astype(BF16).reshape(4, 128, 128)
-        )
-        return carry
-
-    lax.fori_loop(0, 4, backward, 0)
-    tag_row = iota((16, 128), 0)
-
-    def fill(q, carry):
-        count = jnp.int32(0)
-        pairs = [jnp.int32(0), jnp.int32(0)]
-        tags = [jnp.int32(-1), jnp.int32(-1)]
-        for i in range(16):
-            named = part_ref[i // 4, i % 4] == q
-            for s in range(2):
-                taken = named & (count == s)
-                pairs[s] = jnp.where(taken, i, pairs[s])
-                tags[s] = jnp.where(taken, block_ref[i // 4, i % 4], tags[s])
-            count = count + jnp.where(named, 1, 0)
-        halo_out[q, 0:128, :] = parts[pairs[0]]
-        halo_out[q, 128:256, :] = parts[pairs[1]]
-        halo_out[q, 256:272, :] = jnp.where(
-            tag_row == 0, tags[0].astype(F32), tags[1].astype(F32)
-        ).astype(BF16)
-        return carry
-
-    lax.fori_loop(0, 16, fill, 0)
-    halo_in[pl.ds(dom, 1)] = halo_out[pl.ds(dom, 1)]
-    send_halo(halo_out, halo_in, one_sem.at[2], one_sem.at[3])
-    lane4 = iota((1, 128), 1) >> 5
-    tall = iota((1024, 128), 0)
-
-    def heat(t, carry):
-        names = asked[pl.ds(t * 16, 16)].reshape(16, 128) & 1023
-        for i in range(4):
-            mixed = names[4 * i : 4 * i + 1, :]
-            for k in range(1, 4):
-                mixed = jnp.where(lane4 == k, names[4 * i + k : 4 * i + k + 1, :], mixed)
-            rows_hot[t, :, i * 128 : (i + 1) * 128] = jnp.where(tall == mixed, 1.0, 0.0).astype(
-                BF16
-            )
-        return carry
-
-    lax.fori_loop(0, 8, heat, 0)
-    wait_recv(15, halo_out, halo_in, one_sem.at[2], one_sem.at[3])
-
-    def collect(c, carry):
-        total = d_self[c]
-        here = c.astype(F32)
-        for q in range(16):
-            tags = halo_in[q, 256:272, :].astype(F32)
-            for s in range(2):
-                piece = halo_in[q, s * 128 : (s + 1) * 128, :].astype(F32)
-                total = total + jnp.where(tags[s : s + 1, :] == here, piece, 0.0)
-        d_self[c] = total
-        return carry
-
-    lax.fori_loop(0, 4, collect, 0)
+    for half in range(2):
+        wait_recv(
+            15,
+            halo_out.at[half],
+            halo_in.at[half],
+            one_sem.at[2 + 4 * half],
+            one_sem.at[3 + 4 * half],
+        )
+        rows = slice(half * 64, half * 64 + 64)
+
+        def collect(c, carry):
+            total = d_self[c, rows, :]
+            for q in range(16):
+                for s in range(2):
+                    total = total + jnp.where(
+                        asked[8 + s, q] == c, halo_in[half, q, s].astype(F32), 0.0
+                    )
+            d_self[c, rows, :] = total
+            return carry
+
+        lax.fori_loop(0, 4, collect, 0)
     d_feature = d_self[...].reshape(512, 128).astype(BF16)
 
     def spread(step, carry):
@@ -469,45 +561,68 @@
 
     lax.fori_loop(0, 8, spread, 0)
     in_grads[pl.ds(me, 1)] = out_rows[pl.ds(me, 1)]
-    wait_send(15, halo_out, halo_in, one_sem.at[2], one_sem.at[3])
-
-    for g in range(4):
+    for half in range(2):
+        wait_send(
+            15,
+            halo_out.at[half],
+            halo_in.at[half],
+            one_sem.at[2 + 4 * half],
+            one_sem.at[3 + 4 * half],
+        )
+
+    for g in range(3):
         wait_recv(31 if g == 0 else 32, out_rows, in_grads, grads_send, grads_recv.at[g])
-        there = [lax.rem(table_id - 2 * g - i + 8, 8) for i in range(2)]
         for i in range(2):
-            onehot[:, i * 512 : (i + 1) * 512] = rows_hot[there[i]]
-
-        def add(c2, carry):
-            for i in range(2):
-                for r in range(8):
-                    start = pl.multiple_of(there[i] * 512 + r * 64, 64)
-                    chunk = row_b[pl.ds(start, 64), :] >> 10
-                    low = i * 512 + r * 64
-                    rows = (
-                        in_grads[pl.ds(there[i] * 16 + r * 2, 2)].reshape(64, 128).astype(F32)
-                    )
-                    for c in range(2):
-                        terms[low : low + 64, c * 128 : (c + 1) * 128] = jnp.where(
-                            chunk == c2 * 2 + c, rows, 0.0
-                        ).astype(BF16)
-            total = dot(onehot[...], terms[...])
+            there = lax.rem(table_id - 2 * g - i + 8, 8)
+            for r in range(8):
+                start = pl.multiple_of(there * 512 + r * 64, 64)
+                chunk = row_b[pl.ds(start, 64), :] >> 10
+                rows = in_grads[pl.ds(there * 16 + r * 2, 2)].reshape(64, 128).astype(F32)
+                low = i * 512 + r * 64
+                for c in range(8):
+                    terms[low : low + 64, c * 128 : (c + 1) * 128] = jnp.where(
+                        chunk == c, rows, 0.0
+                    ).astype(BF16)
+        for c2 in range(4):
+            total = dot(rows_hot[g], terms[:, c2 * 256 : (c2 + 1) * 256])
             for c in range(2):
-                rows = pl.ds(pl.multiple_of((c2 * 2 + c) * 1024, 1024), 1024)
+                start = (c2 * 2 + c) * 1024
                 if g == 0:
-                    table[rows, :] = total[:, c * 128 : (c + 1) * 128]
+                    table[start : start + 1024, :] = total[:, c * 128 : (c + 1) * 128]
                 else:
-                    table[rows, :] += total[:, c * 128 : (c + 1) * 128]
-            if g == 3:
-                rows = pl.ds(pl.multiple_of(c2 * 2048, 2048), 2048)
-                pltpu.make_async_copy(table.at[rows], grad_hbm.at[rows], grad_sem.at[c2]).start()
-            return carry
-
-        lax.fori_loop(0, 4, add, 0)
+                    table[start : start + 1024, :] += total[:, c * 128 : (c + 1) * 128]
+    saves.append(pltpu.make_async_copy(table, sums_hbm, grad_sem.at[3]))
+    saves[-1].start()
+    wait_recv(32, out_rows, in_grads, grads_send, grads_recv.at[3])
+    for i in range(2):
+        saves.append(
+            pltpu.make_async_copy(
+                in_grads.at[pl.ds(last[i] * 16, 16)],
+                late_hbm.at[pl.ds(i * 16, 16)],
+                grad_sem.at[4 + i],
+            )
+        )
+        saves[-1].start()
     wait_send(127, out_rows, in_grads, grads_send, grads_recv.at[0])
     store.wait()
-    for c2 in range(4):
-        rows = pl.ds(c2 * 2048, 2048)
-        pltpu.make_async_copy(table.at[rows], grad_hbm.at[rows], grad_sem.at[c2]).wait()
+    for save in saves:
+        save.wait()
+
+
+def last_kernel(hot, row_b, late, sums, node, grad, node_out, terms):
+    c2 = pl.program_id(0)
+    node_out[...] = node[...]
+    for r in range(16):
+        chunk = row_b[r * 64 : (r + 1) * 64, :] >> 10
+        rows = late[2 * r : 2 * r + 2].reshape(64, 128).astype(F32)
+        for c in range(2):
+            terms[r * 64 : (r + 1) * 64, c * 128 : (c + 1) * 128] = jnp.where(
+                chunk == c2 * 2 + c, rows, 0.0
+            ).astype(BF16)
+    total = dot(hot[...], terms[...])
+    for c in range(2):
+        part = slice(c * 1024, (c + 1) * 1024)
+        grad[part, :] = sums[part, :] + total[:, c * 128 : (c + 1) * 128]
 
 
 def body(
@@ -530,12 +645,18 @@
     held = [pl.BlockSpec(memory_space=pltpu.VMEM)]
     scalar = [pl.BlockSpec(memory_space=pltpu.SMEM)]
     anywhere = [pl.BlockSpec(memory_space=pl.ANY)]
-    node_out, table_grad = pl.pallas_call(
+    node, sums, hot, low, late = pl.pallas_call(
         step_kernel,
         name="step",
-        out_shape=(shape((512, 1024), BF16), shape((8192, 128), F32)),
+        out_shape=(
+            shape((512, 1024), BF16),
+            shape((8192, 128), F32),
+            shape((1024, 1024), BF16),
+            shape((1024, 128), jnp.int32),
+            shape((32, 32, 128), BF16),
+        ),
         in_specs=held * 2 + scalar * 2 + held * 2 + anywhere * 6,
-        out_specs=tuple(anywhere * 2),
+        out_specs=tuple(anywhere * 5),
         scratch_shapes=[
             vmem((8192, 128), F32),
             vmem((1024, 1024), BF16),
@@ -545,8 +666,9 @@
             vmem((512, 1024), BF16),
             vmem((512, 1024), BF16),
             vmem((1024, 1024), BF16),
-            vmem((128, 1, 128), jnp.int32),
-            vmem((128, 1, 128), jnp.int32),
+            vmem((8, 16, 1, 128), jnp.int32),
+            vmem((10, 16, 1, 128), jnp.int32),
+            vmem((10, 16, 1, 128), jnp.int32),
             vmem((128, 512), F32),
             vmem((4096, 128), jnp.int32),
             vmem((128, 32, 128), BF16),
@@ -566,20 +688,20 @@
             vmem((512, 1024), BF16),
             vmem((4, 128, 1024), BF16),
             vmem((4, 128, 128), F32),
-            vmem((16, 128, 128), BF16),
-            vmem((16, 272, 128), BF16),
-            vmem((16, 272, 128), BF16),
-            vmem((8, 1024, 512), BF16),
-            vmem((1024, 256), BF16),
+            vmem((16, 64, 128), BF16),
+            vmem((2, 16, 2, 64, 128), BF16),
+            vmem((2, 16, 2, 64, 128), BF16),
+            vmem((4, 1024, 1024), BF16),
+            vmem((1024, 1024), BF16),
             dma((7,)),
-            dma((4,)),
+            dma((8,)),
             dma,
             dma((4,)),
             dma,
             dma((4,)),
             dma((2, 20)),
             dma((2, 20)),
-            dma((4,)),
+            dma((6,)),
         ],
         compiler_params=pltpu.CompilerParams(
             collective_id=0, has_side_effects=True, vmem_limit_bytes=LIMIT
@@ -598,6 +720,23 @@
         adjacency,
         cotangent,
     )
+    table_grad, node_out = pl.pallas_call(
+        last_kernel,
+        name="last",
+        grid=(4,),
+        out_shape=(shape((8192, 128), F32), shape((512, 1024), BF16)),
+        in_specs=held * 3
+        + [
+            pl.BlockSpec((2048, 128), lambda c: (c, 0)),
+            pl.BlockSpec((128, 1024), lambda c: (c, 0)),
+        ],
+        out_specs=(
+            pl.BlockSpec((2048, 128), lambda c: (c, 0)),
+            pl.BlockSpec((128, 1024), lambda c: (c, 0)),
+        ),
+        scratch_shapes=[vmem((1024, 256), BF16)],
+        compiler_params=pltpu.CompilerParams(vmem_limit_bytes=LIMIT),
+    )(hot, low, late, sums, node)
     return (node_out, table_grad[None])
 
 

time: 125 us -> 112 us (0.90)
  the two profiles are of different devices: /device:TPU:13 before, /device:TPU:1 now
where the time goes in v3:
time: 112 us
  Pallas kernels  111 us (99%)
    pallas_call x1, Pallas kernels, body(): pl.pallas_call(step_kernel, name='step', out_shape=(shape((512, 1024), BF...  104 us
    pallas_call x1, Pallas kernels, body(): pl.pallas_call(last_kernel, name='last', grid=(4,), out_shape=(shape((819...  7.55 us

profile of v3, /device:TPU:1, one launch (start us, length us, event | category | flops | bytes accessed | tf_op | source)
XLA Modules:
  0.0 111.9 jit_solution(1897439797320796530)
XLA Ops:
  0.6 103.8 %step.1 = (bf16[512,1024]{1,0:T(8,128)(2,1)}, f32[8192,128]{1,0:T(8,128)}, bf16[1024,1024]{1,0:T(8,128)(2,1)}, s32[1024,128]{1,0:T(8,128)}, bf16[32,32,128]{2,1,0:T(8,128)(2,1)}) custom-call(s32[4,512]{1,0:T(4,128)} %bitcast.5, s32[4,512]{1,0:T(4,128)} %bitcast.6, s32[4,4]{1,0:T(4,128)} %part_ref.1, s32[4,4]{1,0:T(4,128)} %block_ref.1, ...), custom_call_target="tpu_custom_call" | custom-call | tf_op jit(solution)/shard_map/step/pallas_call | solution.py:648
  104.4 7.5 %last.1 = (f32[8192,128]{1,0:T(8,128)}, bf16[512,1024]{1,0:T(8,128)(2,1)}) custom-call(bf16[1024,1024]{1,0:T(8,128)(2,1)} %get-tuple-element.9.hot, s32[1024,128]{1,0:T(8,128)} %get-tuple-element.10.row_b, bf16[32,32,128]{2,1,0:T(8,128)(2,1)} %get-tuple-element.11.late, f32[8192,128]{1,0:T(8,128)} %get-tuple-element.12.sums, ...), custom_call_target="tpu_custom_call" | custom-call | tf_op jit(solution)/shard_map/last/pallas_call | solution.py:723

commit v4 on v3

--- a/solution.py
+++ b/solution.py
@@ -450,7 +450,7 @@
     gain = gain_ref[...].astype(F32).reshape(1, 1024)
 
     def norm(r, carry):
-        rows = pl.ds(pl.multiple_of(r * 32, 32), 32)
+        rows = pl.ds(pl.multiple_of(r * 64, 64), 64)
         pre = pre_act[rows, :]
         s = jax.nn.sigmoid(pre)
         active = pre * s
@@ -463,7 +463,7 @@
         d_pre[rows, :] = (d_active * (s * (1.0 + pre * (1.0 - s)))).astype(BF16)
         return carry
 
-    lax.fori_loop(0, 16, norm, 0)
+    lax.fori_loop(0, 8, norm, 0)
     store = pltpu.make_async_copy(node_out, node_out_hbm, load_sem.at[6])
     store.start()
     d_mean = dot(d_pre[...], w_neigh[...], NT)

time: 112 us -> 111 us (level)
  no operation moved by 1% of the time
where the time goes in v4:
time: 111 us
  Pallas kernels  111 us (100%)
    pallas_call x1, Pallas kernels, body(): pl.pallas_call(step_kernel, name='step', out_shape=(shape((512, 1024), BF...  103 us
    pallas_call x1, Pallas kernels, body(): pl.pallas_call(last_kernel, name='last', grid=(4,), out_shape=(shape((819...  7.55 us

profile of v4, /device:TPU:1, one launch (start us, length us, event | category | flops | bytes accessed | tf_op | source)
XLA Modules:
  0.0 111.2 jit_solution(3060624252827918415)
XLA Ops:
  0.6 103.0 %step.1 = (bf16[512,1024]{1,0:T(8,128)(2,1)}, f32[8192,128]{1,0:T(8,128)}, bf16[1024,1024]{1,0:T(8,128)(2,1)}, s32[1024,128]{1,0:T(8,128)}, bf16[32,32,128]{2,1,0:T(8,128)(2,1)}) custom-call(s32[4,512]{1,0:T(4,128)} %bitcast.5, s32[4,512]{1,0:T(4,128)} %bitcast.6, s32[4,4]{1,0:T(4,128)} %part_ref.1, s32[4,4]{1,0:T(4,128)} %block_ref.1, ...), custom_call_target="tpu_custom_call" | custom-call | tf_op jit(solution)/shard_map/step/pallas_call | solution.py:648
  103.7 7.5 %last.1 = (f32[8192,128]{1,0:T(8,128)}, bf16[512,1024]{1,0:T(8,128)(2,1)}) custom-call(bf16[1024,1024]{1,0:T(8,128)(2,1)} %get-tuple-element.9.hot, s32[1024,128]{1,0:T(8,128)} %get-tuple-element.10.row_b, bf16[32,32,128]{2,1,0:T(8,128)(2,1)} %get-tuple-element.11.late, f32[8192,128]{1,0:T(8,128)} %get-tuple-element.12.sums, ...), custom_call_target="tpu_custom_call" | custom-call | tf_op jit(solution)/shard_map/last/pallas_call | solution.py:723
